TPU v7x, 32 devices: a whole 2x2x4 slice. The times are simulated.
32 devices in a mesh: row: 16 (over z, x, core), col: 2 (over y).
Axes of the slice: x: 2, y: 2, z: 4, core: 2. Of those that a mesh axis runs over, the one named last changes fastest.
Arguments:
- target_images: float32 [512, 3, 1024], P(('row', 'col')), may hold values from -6 to 6
- target_labels: int32 [512], P(('row', 'col')), may hold values from 0 to 9
- support_images: float32 [128, 3, 1024], P('col'), may hold values from -6 to 6
- support_labels: float32 [128, 10], replicated, may hold values from -3 to 3
- panel_order: int32 [128], replicated, may hold values from 0 to 127, each once
Outputs:
- loss_value: float32 [], replicated
- grad_support: float32 [128, 3, 1024], P('col')
- grad_labels: float32 [128, 10], replicated
Inputs may be any that keep to these rules, and one draw needn't show every extreme that they name: `panel_order`: every support index appears exactly once.
All inputs are finite; a program needn't handle non-finite values.
Results may differ from a plain program's by a relative error of at most 0.0003.
Values sent between devices are 32-bit elements; how exact they have to be, the bound alone decides.
A program may use at most 256 MiB of HBM per device.

v0:
```python
import math

import jax
import jax.numpy as jnp
from jax import lax
from jax.sharding import PartitionSpec as P

SIDE = 32
CLASSES = 10


JITTER = 0.1
RIDGE = 0.01


def shifted(planes, stride):
    filler = jnp.zeros(planes.shape[:-1] + (abs(stride),), planes.dtype)
    if stride > 0:
        return jnp.concatenate([planes[..., stride:], filler], axis=-1)
    return jnp.concatenate([filler, planes[..., :stride]], axis=-1)


def window(planes, side_len):
    column = jnp.arange(planes.shape[-1], dtype=jnp.int32) % side_len
    across = planes + jnp.where(column < side_len - 1, shifted(planes, 1), 0.0)
    across = across + jnp.where(column > 0, shifted(planes, -1), 0.0)
    return (across + shifted(across, side_len) + shifted(across, -side_len)) / 9.0


def rectify(covariance, first_diag, second_diag):
    scales = jnp.sqrt((first_diag + JITTER) * (second_diag + JITTER))
    cosine = covariance / scales
    angles = jnp.arccos(cosine)
    energy = scales * (jnp.sqrt(1.0 - cosine * cosine) + (math.pi - angles) * cosine) / math.pi
    return (energy, (math.pi - angles) / math.pi)


def self_maps(images, side_len):
    first_diag = window(jnp.mean(images * images, axis=1), side_len)
    energy, unused = rectify(first_diag, first_diag, first_diag)
    return (first_diag, window(energy, side_len))


def pair_kernel(first_images, second_images, first_maps, second_maps, side_len):
    products = first_images[:, None, 0] * second_images[None, :, 0]
    for channel in range(1, first_images.shape[1]):
        products = products + first_images[:, None, channel] * second_images[None, :, channel]
    first_sigma = window(products / first_images.shape[1], side_len)
    first_energy, first_slope = rectify(
        first_sigma, first_maps[0][:, None], second_maps[0][None, :]
    )
    second_sigma = window(first_energy, side_len)
    tangent = window(first_energy + first_slope * first_sigma, side_len)
    second_energy, second_slope = rectify(
        second_sigma, first_maps[1][:, None], second_maps[1][None, :]
    )
    return jnp.mean(second_energy + second_slope * tangent, axis=-1)


def pair_parts(first_images, second_images, first_maps, second_maps, side_len):
    products = first_images[:, None, 0] * second_images[None, :, 0]
    for channel in range(1, first_images.shape[1]):
        products = products + first_images[:, None, channel] * second_images[None, :, channel]
    first_sigma = window(products / first_images.shape[1], side_len)
    first_scales = jnp.sqrt((first_maps[0][:, None] + JITTER) * (second_maps[0][None, :] + JITTER))
    first_cos = first_sigma / first_scales
    first_energy, first_slope = rectify(
        first_sigma, first_maps[0][:, None], second_maps[0][None, :]
    )
    second_sigma = window(first_energy, side_len)
    tangent = window(first_energy + first_slope * first_sigma, side_len)
    second_scales = jnp.sqrt((first_maps[1][:, None] + JITTER) * (second_maps[1][None, :] + JITTER))
    second_cos = second_sigma / second_scales
    second_energy, second_slope = rectify(
        second_sigma, first_maps[1][:, None], second_maps[1][None, :]
    )
    values = jnp.mean(second_energy + second_slope * tangent, axis=-1)
    return (values, first_sigma, first_cos, tangent, second_cos)


def pair_pullback(
    first_images,
    first_maps,
    second_images,
    second_maps,
    first_sigma,
    first_cos,
    tangent,
    second_cos,
    cotangent,
    side_len,
):
    highest = lax.Precision.HIGHEST
    pixels = first_sigma.shape[-1]
    weight = cotangent[:, :, None] / pixels
    second_far = second_maps[1][None, :] + JITTER
    second_scales = jnp.sqrt((first_maps[1][:, None] + JITTER) * second_far)
    second_sine = jnp.sqrt(1.0 - second_cos * second_cos)
    second_slope = (math.pi - jnp.arccos(second_cos)) / math.pi
    grad_tangent = weight * second_slope
    grad_cos2 = weight * tangent / (math.pi * second_sine)
    grad_sigma2 = weight * second_slope + grad_cos2 / second_scales
    grad_scale2 = weight * second_sine / math.pi - grad_cos2 * second_cos / second_scales
    grad_q2 = jnp.sum(grad_scale2 * second_scales / (2.0 * second_far), axis=0)
    first_far = second_maps[0][None, :] + JITTER
    first_scales = jnp.sqrt((first_maps[0][:, None] + JITTER) * first_far)
    first_sine = jnp.sqrt(1.0 - first_cos * first_cos)
    first_slope = (math.pi - jnp.arccos(first_cos)) / math.pi
    grad_inner = window(grad_tangent, side_len)
    grad_energy = window(grad_sigma2, side_len) + grad_inner
    grad_cos1 = grad_inner * first_sigma / (math.pi * first_sine)
    grad_sigma1 = grad_inner * first_slope + grad_energy * first_slope + grad_cos1 / first_scales
    grad_scale1 = grad_energy * first_sine / math.pi - grad_cos1 * first_cos / first_scales
    grad_q1 = jnp.sum(grad_scale1 * first_scales / (2.0 * first_far), axis=0)
    grad_products = window(grad_sigma1, side_len) / first_images.shape[1]
    direct = jnp.einsum("abp,acp->bcp", grad_products, first_images, precision=highest)
    unused, maps_pull = jax.vjp(lambda images: self_maps(images, side_len), second_images)
    return direct + maps_pull((grad_q1, grad_q2))[0]


def order_matrix(panel_order, blocks):
    return (panel_order[:, None] == jnp.arange(blocks, dtype=jnp.int32)[None, :]).astype(
        jnp.float32
    )


def to_stored(labels, matrix):
    return jnp.dot(matrix, labels, precision=lax.Precision.HIGHEST)


def to_logical(labels, matrix):
    return jnp.dot(matrix.T, labels, precision=lax.Precision.HIGHEST)


def ridge_factor(kernel):
    number = kernel.shape[0]
    ridge_term = RIDGE * jnp.trace(kernel) / number
    return jnp.linalg.cholesky(kernel + ridge_term * jnp.eye(number, dtype=kernel.dtype))


def ridge_solve(factor, rhs):
    middle = lax.linalg.triangular_solve(factor, rhs, left_side=True, lower=True)
    return lax.linalg.triangular_solve(factor, middle, left_side=True, lower=True, transpose_a=True)


def add_rows(running, values, offset):
    current = lax.dynamic_slice_in_dim(running, offset, values.shape[0], 0)
    return lax.dynamic_update_slice_in_dim(running, current + values, offset, 0)


def local(target_images, target_labels, support_images, support_labels, panel_order):
    highest = lax.Precision.HIGHEST
    row_count = lax.axis_size("row")
    col_count = lax.axis_size("col")
    row_index = lax.axis_index("row")
    col_index = lax.axis_index("col")
    panel_size = support_images.shape[0]
    support = panel_size * col_count
    per_row = support // row_count
    targets_dev = target_images.shape[0]
    channels = target_images.shape[1]
    pixels = target_images.shape[2]
    target_maps = self_maps(target_images, SIDE)
    shard_piece = lax.all_gather(support_images, "col", axis=0, tiled=True)
    piece_maps = self_maps(shard_piece, SIDE)
    values, sigma, cos_one, tangent, cos_two = pair_parts(
        target_images, shard_piece, target_maps, piece_maps, SIDE
    )
    kernel_ts = values
    absorb_first_diag = piece_maps[0]
    absorb_second_diag = piece_maps[1]
    absorb_sigma_maps = sigma
    absorb_cos_first = cos_one
    absorb_tangent_maps = tangent
    absorb_cos_second = cos_two
    (
        kernel_ts,
        gathered,
        first_diag,
        second_diag,
        sigma_maps,
        cos_first,
        tangent_maps,
        cos_second,
    ) = (
        kernel_ts,
        shard_piece,
        absorb_first_diag,
        absorb_second_diag,
        absorb_sigma_maps,
        absorb_cos_first,
        absorb_tangent_maps,
        absorb_cos_second,
    )
    own_start = col_index * panel_size
    partner_start = row_index * per_row
    own_maps = (
        lax.dynamic_slice_in_dim(first_diag, own_start, panel_size, 0),
        lax.dynamic_slice_in_dim(second_diag, own_start, panel_size, 0),
    )
    partner = lax.dynamic_slice_in_dim(gathered, partner_start, per_row, 0)
    partner_maps = (
        lax.dynamic_slice_in_dim(first_diag, partner_start, per_row, 0),
        lax.dynamic_slice_in_dim(second_diag, partner_start, per_row, 0),
    )
    kss_block = pair_kernel(support_images, partner, own_maps, partner_maps, SIDE)
    padded = lax.dynamic_update_slice(
        jnp.zeros((support, support), jnp.float32), kss_block, (own_start, partner_start)
    )
    wanted = (target_labels[:, None] == jnp.arange(CLASSES, dtype=jnp.int32)[None, :]).astype(
        jnp.float32
    ) - 0.1
    matrix = order_matrix(panel_order, support)
    stored_labels = to_stored(support_labels, matrix)
    total_targets = targets_dev * row_count * col_count
    kernel_ss = lax.psum(padded, ("row", "col"))
    factor = ridge_factor(kernel_ss)
    alphas = ridge_solve(factor, stored_labels)
    residual = jnp.dot(kernel_ts, alphas, precision=highest) - wanted
    alpha_grad, squared = lax.psum(
        (jnp.dot(kernel_ts.T, residual, precision=highest), jnp.sum(residual * residual)),
        ("row", "col"),
    )
    loss_value = 0.5 * squared / total_targets
    adjoint = ridge_solve(factor, alpha_grad)
    kss_grad = -jnp.dot(adjoint, alphas.T, precision=highest) - RIDGE / support * jnp.sum(
        adjoint * alphas
    ) * jnp.eye(support, dtype=jnp.float32)
    kts_grad = jnp.dot(residual, alphas.T, precision=highest)

    def own_kernel(own_images, partner_images):
        return pair_kernel(
            own_images,
            partner_images,
            self_maps(own_images, SIDE),
            self_maps(partner_images, SIDE),
            SIDE,
        )

    unused, pullback = jax.vjp(own_kernel, support_images, partner)
    own_grad, partner_grad = pullback(
        lax.dynamic_slice(kss_grad, (own_start, partner_start), (panel_size, per_row))
    )
    gradient = jnp.zeros((support, channels, pixels), jnp.float32)
    gradient = add_rows(gradient, own_grad, own_start)
    gradient = add_rows(gradient, partner_grad, partner_start)

    def panel_step(panel_number, running):
        offset = panel_number * panel_size
        images = lax.dynamic_slice_in_dim(gathered, offset, panel_size, 0)
        panel_maps = (
            lax.dynamic_slice_in_dim(first_diag, offset, panel_size, 0),
            lax.dynamic_slice_in_dim(second_diag, offset, panel_size, 0),
        )
        cotangent = lax.dynamic_slice_in_dim(kts_grad, offset, panel_size, 1)
        sigma = lax.dynamic_slice_in_dim(sigma_maps, offset, panel_size, 1)
        cos_one = lax.dynamic_slice_in_dim(cos_first, offset, panel_size, 1)
        tangent = lax.dynamic_slice_in_dim(tangent_maps, offset, panel_size, 1)
        cos_two = lax.dynamic_slice_in_dim(cos_second, offset, panel_size, 1)
        values = pair_pullback(
            target_images,
            target_maps,
            images,
            panel_maps,
            sigma,
            cos_one,
            tangent,
            cos_two,
            cotangent,
            SIDE,
        )
        return add_rows(running, values, offset)

    gradient = lax.fori_loop(0, col_count, panel_step, gradient)
    summed = lax.psum(gradient, ("row", "col"))
    grad_support = lax.dynamic_slice_in_dim(summed, own_start, panel_size, 0)
    return (loss_value, grad_support, to_logical(adjoint, matrix))


def solution(mesh):
    placed = (P(("row", "col"), None, None), P(("row", "col")), P("col", None, None), P(), P())
    return jax.shard_map(
        local,
        mesh=mesh,
        in_specs=placed,
        out_specs=(P(), P("col", None, None), P()),
        check_vma=False,
    )
```

profile of v0, /device:TPU:0, one launch (start us, length us, event | category | flops | bytes accessed | tf_op | source)
XLA Modules:
  0.0 993.9 jit_solution(16178696438533514220)
XLA Ops:
  25.7 13.9 %all-gather.2.cloned.1.call-done = f32[128,3,1024]{2,0,1:T(8,128)} async-done(((f32[64,3,1024]{2,0,1:T(8,128)}), f32[128,3,1024]{2,0,1:T(8,128)}) %all-gather.2.cloned.1.call-update) | async-done | bytes 1572880 | tf_op jit(solution)/shard_map/all_gather | solution.py:164
  43.1 2.4 multiply_multiply_fusion.4
  45.7 2.5 select_add_fusion.12
  54.1 2.6 slice_bitcast_fusion.2
  56.7 2.1 copy.67
  58.8 2.1 copy.69
  60.9 2.0 copy.71
  62.9 7.9 add_multiply_fusion.4
  70.8 6.5 fusion.92
  77.3 13.5 %select_add_fusion.6 = f32[16,128,1024]{1,0,2:T(8,128)S(1)} fusion(f32[16,128,1023]{1,0,2:T(8,128)} %get-tuple-element.482, f32[16,128,1023]{1,0,2:T(8,128)} %get-tuple-element.481, pred[1024]{0:T(1024)(128)(4,1)S(1)} %get-tuple-element.607, pred[1024]{0:T(1024)(128)(4,1)S(1)} %get-tuple-element.608, f32[128,1024]{0,1:T(8,128)S(1)} %copy-done.20, ...), kind=kLoop, calls=%fused_computation.78 | loop fusion | flops 20971520 | bytes 26920960 | tf_op jit(solution)/shard_map/add | solution.py:26
  90.8 6.4 fusion.91
  97.2 13.0 %fusion.24 = (f32[16,128,1024]{1,0,2:T(8,128)}, f32[16,128,1024]{1,0,2:T(8,128)S(1)}) fusion(f32[128,1024]{0,1:T(8,128)S(1)} %copy.65, f32[16,1024]{0,1:T(8,128)S(1)} %copy.64, f32[16,128,992]{1,0,2:T(8,128)} %get-tuple-element.480, f32[16,128,1024]{1,0,2:T(8,128)S(1)} %select_add_fusion.6, f32[16,128,992]{1,0,2:T(8,128)} %get-tuple-element.479), kind=kLoop, calls=%fused_computation.81 | loop fusion | flops 10485760 | bytes 42008576 | tf_op jit(solution)/shard_map/div | solution.py:32
  110.3 25.3 %multiply_add_fusion.2 = (f32[16,128,1024]{1,0,2:T(8,128)S(1)}, f32[16,128,1024]{1,0,2:T(8,128)}) fusion(f32[16,128,1024]{1,0,2:T(8,128)S(1)} %get-tuple-element.786, f32[128,1024]{0,1:T(8,128)S(1)} %copy.65, f32[16,1024]{0,1:T(8,128)S(1)} %copy.64), kind=kLoop, calls=%fused_computation.72 | loop fusion | flops 31457280 | bytes 25755648 | tf_op jit(solution)/shard_map/add | solution.py:71
  135.6 6.8 fusion.88
  143.9 11.2 %fusion.90 = (f32[16,128,1023]{1,0,2:T(8,128)}, f32[16,128,1023]{1,0,2:T(8,128)}) fusion(f32[16,128,1024]{1,0,2:T(8,128)} %get-tuple-element.470), kind=kLoop, calls=%fused_computation.308 | loop fusion | bytes 33521664 | tf_op jit(solution)/shard_map/slice | solution.py:19
  155.2 32.6 %select_add_fusion.4 = (f32[16,128,1024]{1,0,2:T(8,128)}, f32[16,128,1024]{1,0,2:T(8,128)}) fusion(f32[16,128,1023]{1,0,2:T(8,128)} %get-tuple-element.474, f32[16,128,1024]{1,0,2:T(8,128)} %copy-done.4, f32[16,128,1023]{1,0,2:T(8,128)} %get-tuple-element.473, pred[1024]{0:T(1024)(128)(4,1)S(1)} %get-tuple-element.607, ...), kind=kLoop, calls=%fused_computation.71 | loop fusion | flops 41943040 | bytes 67667968 | tf_op jit(solution)/shard_map/add | solution.py:26
  187.8 12.3 %fusion.87 = (f32[16,128,992]{1,0,2:T(8,128)}, f32[16,128,992]{1,0,2:T(8,128)}) fusion(f32[16,128,1024]{1,0,2:T(8,128)} %get-tuple-element.601), kind=kLoop, calls=%fused_computation.305 | loop fusion | bytes 32505856 | tf_op jit(solution)/shard_map/slice | solution.py:19
  201.7 6.5 fusion.89
  214.0 5.7 multiply_multiply_fusion.2
  219.7 5.5 multiply_multiply_fusion.3
  227.0 12.2 %select_add_fusion.10 = (f32[64,8,1024]{2,1,0:T(8,128)S(1)}, f32[64,8,1024]{2,1,0:T(8,128)S(1)}, f32[64,8,1024]{2,1,0:T(8,128)S(1)}, f32[64,8,1024]{2,1,0:T(8,128)S(1)}) fusion(f32[64,8,1023]{2,1,0:T(8,128)S(1)} %get-tuple-element.514, f32[64,8,1023]{2,1,0:T(8,128)S(1)} %get-tuple-element.513, pred[1024]{0:T(1024)(128)(4,1)S(1)} %get-tuple-element.607, ...), kind=kLoop, calls=%fused_computation.139 | loop fusion | flops 19922944 | bytes 19458048 | tf_op jit(solution)/shard_map/add | solution.py:26
  240.9 3.1 select_add_fusion.7
  245.9 6.7 add_reduce_fusion.1
  254.1 5.1 fusion.96
  259.2 2.9 fusion.98
  263.1 31.9 %add_reduce_fusion = (f32[16,128]{1,0:T(8,128)S(1)}, f32[16,128,1024]{1,0,2:T(8,128)}, f32[16,128,1024]{1,0,2:T(8,128)}) fusion(f32[128,1024]{0,1:T(8,128)S(1)} %copy.63, f32[16,1024]{0,1:T(8,128)S(1)} %copy-done.28, f32[16,128,992]{1,0,2:T(8,128)} %get-tuple-element.476, f32[16,128,1024]{1,0,2:T(8,128)} %get-tuple-element.602, ...), kind=kLoop, calls=%fused_computation.69 | loop fusion | flops 46135296 | bytes 66658304 | tf_op jit(solution)/shard_map/reduce_sum | solution.py:77
  295.1 76.9 %all-reduce.126.cloned.1.call-done = f32[128,128]{1,0:T(8,128)} async-done(((f32[128,128]{1,0:T(8,128)}), f32[128,128]{1,0:T(8,128)}) %all-reduce.126.cloned.1.call-update) | async-done | bytes 65552 | tf_op jit(solution)/shard_map/psum | solution.py:216
  375.9 11.7 %cholesky.23 = f32[128,128]{1,0:T(8,128)S(1)} custom-call(f32[128,128]{1,0:T(8,128)S(1)} %fusion.53), custom_call_target="Cholesky" | custom-call | tf_op jit(solution)/shard_map/jit(cholesky)/cholesky | solution.py:138
  389.0 9.8 custom-call.12
  400.3 41.1 %all-reduce.122 = (f32[]{:T(128)}, f32[128,10]{0,1:T(8,128)S(1)}) all-reduce(f32[]{:T(128)} %get-tuple-element.603, f32[128,10]{0,1:T(8,128)S(1)} %fusion.65), channel_id=1, replica_groups=mesh['row'=16,'col'=2] {'row','col'}, use_global_device_ids=true, to_apply=%region_9.12 | all-reduce | flops 1281 | bytes 10248 | tf_op jit(solution)/shard_map/psum | solution.py:220
  443.5 10.6 %divide_multiply_fusion = (f32[64,8,1024]{2,1,0:T(8,128)S(1)}, f32[64,8,1024]{2,1,0:T(8,128)S(1)}, f32[64,8,1024]{2,1,0:T(8,128)S(1)}) fusion(f32[64,8]{1,0:T(8,128)S(1)} %get-tuple-element.568, f32[8,1024]{1,0:T(8,128)S(1)} %multiply_add_fusion.8, f32[64,1024]{1,0:T(8,128)S(1)} %copy-done.23, f32[64,8,992]{2,1,0:T(8,128)} %get-tuple-element.508, ...), kind=kLoop, calls=%fused_computation.99 | loop fusion | flops 21495808 | bytes 18911232 | tf_op jit(solution)/shard_map/transpose(jvp())/mul | solution.py:31
  454.1 7.4 multiply_reduce_fusion.1
  467.2 8.7 divide_multiply_fusion.1
  482.1 2.8 multiply_reduce_fusion.5
  488.4 363.0 %while.15 = (s32[]{:T(128)}, f32[128,3,1024]{2,0,1:T(8,128)}, f32[16,128,1024]{1,0,2:T(8,128)}, f32[16,128]{1,0:T(8,128)S(1)}, f32[16,128,1024]{1,0,2:T(8,128)},...) while((s32[]{:T(128)}, f32[128,3,1024]{2,0,1:T(8,128)}, ...), condition=%wide.region_28.31_spmd, body=%wide.region_24.30_spmd.sunk | while | flops 114337536 | bytes 337252384 | solution.py:274
  496.5 29.1 %divide_add_fusion.2 = (f32[16,64,1024]{1,0,2:T(8,128)S(1)}, f32[16,64,1024]{1,0,2:T(8,128)S(1)}, f32[64,1024]{0,1:T(8,128)S(1)}) fusion(f32[16,128,1024]{1,0,2:T(8,128)} %get-tuple-element.817, s32[]{:T(128)S(6)} %select_n.634, f32[16,128,1024]{1,0,2:T(8,128)} %get-tuple-element.814, f32[64,1024]{0,1:T(8,128)S(1)} %get-tuple-element.740, ...), kind=kLoop, calls=%fused_computation.16.clone.1 | loop fusion | flops 23003136 | bytes 17637380 | tf_op jit(solution)/shard_map/while/body/eval_jaxpr/add | solution.py:102
  525.6 6.4 fusion.159
  532.1 6.5 fusion.161
  538.6 19.7 %select_add_fusion.24 = (f32[16,64,1024]{1,0,2:T(8,128)}, f32[16,64,1024]{1,0,2:T(8,128)}) fusion(f32[16,64,1023]{1,0,2:T(8,128)} %get-tuple-element.746, f32[16,64,1024]{1,0,2:T(8,128)S(1)} %get-tuple-element.745, f32[16,64,1023]{1,0,2:T(8,128)} %get-tuple-element.747, pred[1024]{0:T(1024)(128)(4,1)S(1)} %get-tuple-element.748, ...), kind=kLoop, calls=%fused_computation.22.clone.1 | loop fusion | flops 8388608 | bytes 33540096 | tf_op jit(solution)/shard_map/while/body/eval_jaxpr/add | solution.py:26
  558.3 12.3 %fusion.162 = (f32[16,64,992]{1,0,2:T(8,128)}, f32[16,64,992]{1,0,2:T(8,128)}) fusion(f32[16,64,1024]{1,0,2:T(8,128)} %get-tuple-element.753), kind=kLoop, calls=%fused_computation.299.clone.1 | loop fusion | bytes 16252928 | tf_op jit(solution)/shard_map/while/body/eval_jaxpr/slice | solution.py:19
  572.3 6.1 fusion.163
  578.7 37.8 %fusion.164 = (f32[64,1024]{0,1:T(8,128)}, f32[16,64,1024]{1,0,2:T(8,128)}) fusion(f32[16,128,1024]{1,0,2:T(8,128)} %get-tuple-element.816, s32[]{:T(128)S(6)} %select_n.634, f32[16,128,1024]{1,0,2:T(8,128)} %get-tuple-element.820, f32[64,1024]{0,1:T(8,128)S(1)} %get-tuple-element.736, f32[64,1024]{0,1:T(8,128)S(1)} %get-tuple-element.737, ...), kind=kLoop, calls=%fused_computation.25.clone.1 | loop fusion | flops 32440320 | bytes 38076420 | tf_op jit(solution)/shard_map/while/body/eval_jaxpr/reduce_sum | solution.py:114
  618.1 2.2 constant_dynamic-slice_fusion.7
  625.2 2.1 fusion.170
  629.4 6.6 fusion.165
  636.0 7.7 select_add_fusion.25
  643.7 6.5 fusion.166
  653.7 15.5 %fusion.172 = f32[64,3,1024]{0,1,2:T(4,128)} fusion(f32[64,3,1024]{0,1,2:T(4,128)} %copy.94, f32[64,3,1024]{0,1,2:T(4,128)S(1)} %copy.95, f32[16,3,1024]{0,1,2:T(4,128)} %get-tuple-element.823, f32[16,64,992]{1,0,2:T(8,128)} %get-tuple-element.762, f32[16,64,1024]{1,0,2:T(8,128)} %copy-done.2, f32[16,64,992]{1,0,2:T(8,128)} %get-tuple-element.763, ...), kind=kOutput, calls=%fused_computation.28.clone.1 | convolution fusion | flops 41680896 | bytes 15138816 | tf_op jit(solution)/shard_map/while/body/eval_jaxpr/abp,acp->bcp/dot_general | solution.py:116
  669.2 1.9 copy.98
  675.3 29.1 %divide_add_fusion.2 = (f32[16,64,1024]{1,0,2:T(8,128)S(1)}, f32[16,64,1024]{1,0,2:T(8,128)S(1)}, f32[64,1024]{0,1:T(8,128)S(1)}) fusion(f32[16,128,1024]{1,0,2:T(8,128)} %get-tuple-element.817, s32[]{:T(128)S(6)} %select_n.634, f32[16,128,1024]{1,0,2:T(8,128)} %get-tuple-element.814, f32[64,1024]{0,1:T(8,128)S(1)} %get-tuple-element.740, ...), kind=kLoop, calls=%fused_computation.16.clone.1 | loop fusion | flops 23003136 | bytes 17637380 | tf_op jit(solution)/shard_map/while/body/eval_jaxpr/add | solution.py:102
  704.4 6.4 fusion.159
  710.9 6.5 fusion.161
  717.4 19.7 %select_add_fusion.24 = (f32[16,64,1024]{1,0,2:T(8,128)}, f32[16,64,1024]{1,0,2:T(8,128)}) fusion(f32[16,64,1023]{1,0,2:T(8,128)} %get-tuple-element.746, f32[16,64,1024]{1,0,2:T(8,128)S(1)} %get-tuple-element.745, f32[16,64,1023]{1,0,2:T(8,128)} %get-tuple-element.747, pred[1024]{0:T(1024)(128)(4,1)S(1)} %get-tuple-element.748, ...), kind=kLoop, calls=%fused_computation.22.clone.1 | loop fusion | flops 8388608 | bytes 33540096 | tf_op jit(solution)/shard_map/while/body/eval_jaxpr/add | solution.py:26
  737.1 12.3 %fusion.162 = (f32[16,64,992]{1,0,2:T(8,128)}, f32[16,64,992]{1,0,2:T(8,128)}) fusion(f32[16,64,1024]{1,0,2:T(8,128)} %get-tuple-element.753), kind=kLoop, calls=%fused_computation.299.clone.1 | loop fusion | bytes 16252928 | tf_op jit(solution)/shard_map/while/body/eval_jaxpr/slice | solution.py:19
  751.1 6.1 fusion.163
  757.5 37.8 %fusion.164 = (f32[64,1024]{0,1:T(8,128)}, f32[16,64,1024]{1,0,2:T(8,128)}) fusion(f32[16,128,1024]{1,0,2:T(8,128)} %get-tuple-element.816, s32[]{:T(128)S(6)} %select_n.634, f32[16,128,1024]{1,0,2:T(8,128)} %get-tuple-element.820, f32[64,1024]{0,1:T(8,128)S(1)} %get-tuple-element.736, f32[64,1024]{0,1:T(8,128)S(1)} %get-tuple-element.737, ...), kind=kLoop, calls=%fused_computation.25.clone.1 | loop fusion | flops 32440320 | bytes 38076420 | tf_op jit(solution)/shard_map/while/body/eval_jaxpr/reduce_sum | solution.py:114
  797.0 2.2 constant_dynamic-slice_fusion.7
  804.0 2.1 fusion.170
  808.3 6.6 fusion.165
  814.8 7.7 select_add_fusion.25
  822.6 6.5 fusion.166
  832.5 15.5 %fusion.172 = f32[64,3,1024]{0,1,2:T(4,128)} fusion(f32[64,3,1024]{0,1,2:T(4,128)} %copy.94, f32[64,3,1024]{0,1,2:T(4,128)S(1)} %copy.95, f32[16,3,1024]{0,1,2:T(4,128)} %get-tuple-element.823, f32[16,64,992]{1,0,2:T(8,128)} %get-tuple-element.762, f32[16,64,1024]{1,0,2:T(8,128)} %copy-done.2, f32[16,64,992]{1,0,2:T(8,128)} %get-tuple-element.763, ...), kind=kOutput, calls=%fused_computation.28.clone.1 | convolution fusion | flops 41680896 | bytes 15138816 | tf_op jit(solution)/shard_map/while/body/eval_jaxpr/abp,acp->bcp/dot_general | solution.py:116
  852.9 130.8 %all-reduce.128.cloned.1.call-done = f32[128,3,1024]{2,0,1:T(8,128)} async-done(((f32[128,3,1024]{2,0,1:T(8,128)}), f32[128,3,1024]{2,0,1:T(8,128)}) %all-reduce.128.cloned.1.call-update) | async-done | bytes 1572880 | tf_op jit(solution)/shard_map/psum | solution.py:275
  983.7 2.1 constant_dynamic-slice_fusion.4
  (307 shorter events, 105.9 us)
Async XLA Ops:
  7.2 13.3 %copy-start = (f32[128,10]{0,1:T(8,128)S(1)}, f32[128,10]{0,1:T(8,128)}, u32[]{:S(2)}) copy-start(f32[128,10]{0,1:T(8,128)} %param.14) | copy-start | bytes 15364
  7.2 3.9 copy-start.31
  7.2 32.3 %all-gather.2.cloned.1.call-start = ((), (), s32[]{:S(2)}) async-start(), calls=%async_computation | async-start | bytes 2359296 | tf_op jit(solution)/shard_map/all_gather | solution.py:164
  7.9 364.1 %all-reduce.126.cloned.1.call-start = ((), (), s32[]{:S(2)}) async-start(), calls=%async_computation.1 | async-start | bytes 131072 | tf_op jit(solution)/shard_map/psum | solution.py:216
  18.4 2.1 copy-start.43
  20.5 3.4 copy-start.24
  22.0 1.9 copy-start.15
  48.4 5.5 copy-start.30
  53.9 165.8 %copy-start.21 = (f32[64,1024]{1,0:T(8,128)}, f32[64,1024]{1,0:T(8,128)S(1)}, u32[]{:S(2)}) copy-start(f32[64,1024]{1,0:T(8,128)S(1)} %dynamic-slice_add_fusion) | copy-start | bytes 786436
  56.7 6.2 copy-start.17
  70.8 6.5 copy-start.18
  70.8 6.5 copy-start.19
  70.8 6.5 copy-start.20
  110.3 25.3 %copy-start.3 = (f32[16,128,1024]{1,0,2:T(8,128)}, f32[16,128,1024]{1,0,2:T(8,128)S(1)}, u32[]{:S(2)}) copy-start(f32[16,128,1024]{1,0,2:T(8,128)S(1)} %get-tuple-element.786) | copy-start | bytes 25165828
  135.6 8.3 copy-start.4
  187.8 13.9 %copy-start.5 = (f32[16,128,1024]{1,0,2:T(8,128)S(1)}, f32[16,128,1024]{1,0,2:T(8,128)}, u32[]{:S(2)}) copy-start(f32[16,128,1024]{1,0,2:T(8,128)} %get-tuple-element.602) | copy-start | bytes 25165828
  201.7 6.5 copy-start.29
  208.2 2.5 copy-start.26
  208.2 2.5 copy-start.27
  219.7 7.1 copy-start.9
  226.0 1.0 copy-start.22
  244.9 1.0 copy-start.32
  254.0 729.7 %all-reduce.128.cloned.1.call-start = ((), (), s32[]{:S(2)}) async-start(), calls=%async_computation.2 | async-start | bytes 3145728 | tf_op jit(solution)/shard_map/psum | solution.py:275
  254.1 8.1 slice-start.4
  259.2 3.4 slice-start.5
  259.2 3.8 copy-start.28
  263.0 135.8 %copy-start.41 = (f32[128,10]{0,1:T(8,128)S(1)}, f32[128,10]{0,1:T(8,128)}, u32[]{:S(2)}) copy-start(f32[128,10]{0,1:T(8,128)} %fusion.55) | copy-start | bytes 15364
  263.0 136.1 %copy-start.42 = (s32[16]{0:T(128)S(1)}, s32[16]{0:T(128)}, u32[]{:S(2)}) copy-start(s32[16]{0:T(128)} %param.12) | copy-start | bytes 196
  263.0 180.3 %copy-start.38 = (pred[128,128]{1,0:T(8,128)(4,1)S(1)}, pred[128,128]{1,0:T(8,128)(4,1)}, u32[]{:S(2)}) copy-start(pred[128,128]{1,0:T(8,128)(4,1)} %iota_compare_fusion.4) | copy-start | bytes 49156
  263.1 180.4 %copy-start.23 = (f32[64,1024]{1,0:T(8,128)S(1)}, f32[64,1024]{1,0:T(8,128)}, u32[]{:S(2)}) copy-start(f32[64,1024]{1,0:T(8,128)} %multiply_add_fusion.6) | copy-start | bytes 786436
  442.4 11.7 %copy-start.39 = (f32[128,10]{0,1:T(8,128)}, f32[128,10]{0,1:T(8,128)S(1)}, u32[]{:S(2)}) copy-start(f32[128,10]{0,1:T(8,128)S(1)} %get-tuple-element.606) | copy-start | bytes 15364
  464.3 0.9 copy-start.37
  465.3 1.9 copy-start.10
  476.8 1.0 copy-start.25
  480.9 1.1 copy-start.33
  480.9 1.1 copy-start.34
  480.9 1.1 copy-start.35
  484.8 1.1 copy-start.16
  487.1 1.3 copy-start.11
  488.4 363.7 %copy-start.40 = (f32[128,10]{0,1:T(8,128)S(1)}, f32[128,10]{0,1:T(8,128)}, u32[]{:S(2)}) copy-start(f32[128,10]{0,1:T(8,128)} %copy-done.39) | copy-start | bytes 15364
  488.4 363.7 %copy-start.44 = (s32[128]{0:T(128)S(1)}, s32[128]{0:T(128)}, u32[]{:S(2)}) copy-start(s32[128]{0:T(128)} %param.15) | copy-start | bytes 1540
  558.3 12.3 %slice-start.2 = ((s8[8388608]{0:T(1024)(128)(4,1)}), s8[4194304]{0:T(1024)(128)(4,1)S(1)}, s32[]{:S(2)}) async-start(s8[8388608]{0:T(1024)(128)(4,1)} %bitcast.89), calls=%async_computation.5 | async-start | bytes 8388608 | tf_op jit(solution)/shard_map/while
  558.3 14.0 %slice-start.3 = ((s8[8388608]{0:T(1024)(128)(4,1)}), s8[4194304]{0:T(1024)(128)(4,1)S(1)}, s32[]{:S(2)}) async-start(s8[8388608]{0:T(1024)(128)(4,1)} %bitcast.89), calls=%async_computation.6 | async-start | bytes 8388608 | tf_op jit(solution)/shard_map/while
  616.6 1.5 copy-start.12
  623.8 1.0 copy-start.6
  623.8 1.2 copy-start.7
  623.8 1.3 copy-start.8
  623.9 4.0 slice-start
  627.3 2.2 slice-start.1
  643.7 8.2 copy-start.2
  669.2 2.0 copy-start.13
  671.3 1.3 copy-start.14
  737.1 12.3 %slice-start.2 = ((s8[8388608]{0:T(1024)(128)(4,1)}), s8[4194304]{0:T(1024)(128)(4,1)S(1)}, s32[]{:S(2)}) async-start(s8[8388608]{0:T(1024)(128)(4,1)} %bitcast.89), calls=%async_computation.5 | async-start | bytes 8388608 | tf_op jit(solution)/shard_map/while
  737.1 14.0 %slice-start.3 = ((s8[8388608]{0:T(1024)(128)(4,1)}), s8[4194304]{0:T(1024)(128)(4,1)S(1)}, s32[]{:S(2)}) async-start(s8[8388608]{0:T(1024)(128)(4,1)} %bitcast.89), calls=%async_computation.6 | async-start | bytes 8388608 | tf_op jit(solution)/shard_map/while
  795.4 1.5 copy-start.12
  802.6 1.0 copy-start.6
  802.6 1.2 copy-start.7
  802.7 1.3 copy-start.8
  802.7 4.0 slice-start
  806.1 2.2 slice-start.1
  822.5 8.2 copy-start.2
  848.0 2.0 copy-start.13
  850.1 1.3 copy-start.14
  851.4 134.4 %copy-start.1 = (f32[128,10]{0,1:T(8,128)S(1)}, f32[128,10]{0,1:T(8,128)}, u32[]{:S(2)}) copy-start(f32[128,10]{0,1:T(8,128)} %param.14) | copy-start | bytes 15364
  (1 other events, 0.6 us)
Sparse Core Ops, SparseCore 0:
  9.6 29.9 all-gather.1
  254.1 117.8 all-reduce.125
  851.5 132.1 all-reduce.127
where the time goes:
time: 1000 us; the launch traced here: 994 us
  other arithmetic  451 us (45%)
  waiting for transfers between devices  222 us (22%)
  local copies, waits for them, and re-layouts  220 us (22%)
  blocking collectives  41.1 us (4%)
  matrix products  35.4 us (4%)
  between operations  18.1 us (2%)
    slice x48, local copies, waits for them, and re-layouts, shifted(): return jnp.concatenate([planes[..., stride:], filler], axis=-1)  155 us
    psum x1, waiting for transfers between devices, local(): summed = lax.psum(gradient, ('row', 'col'))  131 us
    add x18, other arithmetic, window(): across = across + jnp.where(column > 0, shifted(planes, -1), 0.0)  122 us
    psum x1, waiting for transfers between devices, local(): kernel_ss = lax.psum(padded, ('row', 'col'))  76.9 us
    reduce_sum x2, other arithmetic, pair_pullback(): grad_q1 = jnp.sum(grad_scale1 * first_scales / (2.0 * first_far), axis=0)  75.6 us
    add x2, other arithmetic, pair_pullback(): grad_sigma2 = weight * second_slope + grad_cos2 / second_scales  58.3 us
    psum x1, blocking collectives, local(): lax.psum((jnp.dot(kernel_ts.T, residual, precision=highest), jnp.sum(resi...  41.1 us
    reduce_sum x1, other arithmetic, pair_parts(): values = jnp.mean(second_energy + second_slope * tangent, axis=-1)  31.9 us
  transfers between devices with their start and end apart: 3, of which 3 were waited for; matrix products, arithmetic and copies ran while one was open for 6% of the time, Pallas kernels for 0%

commit v1 on v0

v1 whole, which is shorter than its diff:
```python
import functools
import math

import jax
import jax.numpy as jnp
from jax import lax
from jax.experimental import pallas as pl
from jax.experimental.pallas import tpu as pltpu
from jax.sharding import PartitionSpec as P

SIDE = 32
CLASSES = 10
JITTER = 0.1
RIDGE = 0.01
LANES = 128
SUB = 8
CHUNK = 8
MESH = pl.DeviceIdType.MESH

ACOS = (
    1.5707963050,
    -0.2145988016,
    0.0889789874,
    -0.0501743046,
    0.0308918810,
    -0.0170881256,
    0.0066700901,
    -0.0012624911,
)


def arc(cosine):
    size = jnp.abs(cosine)
    poly = jnp.full_like(size, ACOS[-1] / math.pi)
    for factor in ACOS[-2::-1]:
        poly = poly * size + factor / math.pi
    rest = 1.0 - size
    inverse_root = lax.rsqrt(rest)
    angle = rest * inverse_root * poly
    slope = jnp.where(cosine >= 0.0, 1.0 - angle, angle)
    square = rest * (1.0 + size)
    inverse_sine = lax.rsqrt(square)
    return square * inverse_sine, inverse_sine, slope


def self_energy(diag):
    scale = diag + JITTER
    sine, unused, slope = arc(diag / scale)
    return scale * sine / math.pi + slope * diag, slope + sine / math.pi


def plane_window(values):
    column = lax.broadcasted_iota(jnp.int32, values.shape, 1)
    last = values.shape[1] - 1
    across = values + jnp.where(column < last, pltpu.roll(values, last, 1), 0.0)
    across = across + jnp.where(column > 0, pltpu.roll(values, 1, 1), 0.0)
    zero = jnp.zeros_like(across[:1])
    down = jnp.concatenate([across[1:], zero], axis=0)
    up = jnp.concatenate([zero, across[:-1]], axis=0)
    return (across + down + up) * (1.0 / 9.0)


def lane_window(values):
    lane = lax.broadcasted_iota(jnp.int32, values.shape, 2)
    across = values + pltpu.roll(values, 1, 2) + pltpu.roll(values, LANES - 1, 2)
    across = jnp.where(lane < SIDE, across, 0.0)
    zero = jnp.zeros_like(across[:1])
    down = jnp.concatenate([across[1:], zero], axis=0)
    up = jnp.concatenate([zero, across[:-1]], axis=0)
    return (across + down + up) * (1.0 / 9.0)


def maps_kernel(
    first_ref, second_ref, kernel_ref, prod_ref, q1_ref, q2_ref,
    near_ref, far_ref, one_ref, two_ref, three_ref, four_ref,
):
    channels = first_ref.shape[0]
    pixels = SIDE * SIDE

    @pl.when(pl.program_id(0) == 0)
    def _():
        square = second_ref[0] * second_ref[0]
        for channel in range(1, channels):
            square = square + second_ref[channel] * second_ref[channel]
        diag = plane_window(square * (1.0 / channels))
        far_ref[0] = lax.rsqrt(diag + JITTER)
        far_ref[1] = (diag + JITTER) * lax.rsqrt(diag + JITTER)
        diag = plane_window(self_energy(diag)[0])
        far_ref[2] = lax.rsqrt(diag + JITTER)
        far_ref[3] = (diag + JITTER) * lax.rsqrt(diag + JITTER)
        for ref in (one_ref, two_ref, three_ref, four_ref):
            ref[0] = jnp.zeros(ref.shape[1:], jnp.float32)
            ref[SIDE + 1] = jnp.zeros(ref.shape[1:], jnp.float32)

            def clear(row, carry, ref=ref):
                ref[row, 0] = jnp.zeros((SUB, LANES), jnp.float32)
                ref[row, SIDE + 1] = jnp.zeros((SUB, LANES), jnp.float32)
                return carry

            lax.fori_loop(1, SIDE + 1, clear, 0)

    square = first_ref[0, 0] * first_ref[0, 0]
    for channel in range(1, channels):
        square = square + first_ref[channel, 0] * first_ref[channel, 0]
    diag = lane_window(square * (1.0 / channels))
    near_ref[0] = lax.rsqrt(diag + JITTER)
    near_ref[1] = (diag + JITTER) * lax.rsqrt(diag + JITTER)
    inside = lax.broadcasted_iota(jnp.int32, diag.shape, 2) < SIDE
    diag = lane_window(jnp.where(inside, self_energy(diag)[0], 0.0))
    near_ref[2] = lax.rsqrt(diag + JITTER)
    near_ref[3] = (diag + JITTER) * lax.rsqrt(diag + JITTER)

    def spread(ref, lead, row, start):
        block = ref[lead + (row,)]
        return jnp.stack(
            [jnp.broadcast_to(block[:, x : x + 1], (SUB, LANES)) for x in range(start, start + CHUNK)]
        )

    def across(ref, lead, row, start):
        return jnp.stack(
            [
                jnp.broadcast_to(ref[lead, row, x : x + 1, :], (SUB, LANES))
                for x in range(start, start + CHUNK)
            ]
        )

    def near(index, row, start):
        return spread(near_ref, (index,), row, start)

    def far(index, row, start):
        return across(far_ref, index, row, start)

    def box(ref, row, start):
        width = CHUNK + 2
        tall = (
            ref[row, start : start + width]
            + ref[row + 1, start : start + width]
            + ref[row + 2, start : start + width]
        )
        return tall[:CHUNK] + tall[1 : CHUNK + 1] + tall[2:]

    def put(ref, row, start, values):
        ref[row + 1, start + 1 : start + 1 + CHUNK] = values

    starts = tuple(range(0, SIDE, CHUNK))

    def products(row, carry):
        for start in starts:
            total = spread(first_ref, (0, 0), row, start) * across(second_ref, 0, row, start)
            for channel in range(1, channels):
                total = total + spread(first_ref, (channel, 0), row, start) * across(
                    second_ref, channel, row, start
                )
            put(one_ref, row, start, total)
        return carry

    lax.fori_loop(0, SIDE, products, 0)

    def first_level(row, carry):
        for start in starts:
            sigma = box(one_ref, row, start) * (1.0 / (9.0 * channels))
            cosine = sigma * (near(0, row, start) * far(0, row, start))
            sine, unused, slope = arc(cosine)
            scale = near(1, row, start) * far(1, row, start)
            bent = slope * sigma
            energy = scale * sine * (1.0 / math.pi) + bent
            put(two_ref, row, start, energy)
            put(three_ref, row, start, energy + bent)
            prod_ref[0, row, start : start + CHUNK] = cosine
            q1_ref[0, row, start : start + CHUNK] = slope
        return carry

    lax.fori_loop(0, SIDE, first_level, 0)

    def second_level(row, total):
        for start in starts:
            sigma = box(two_ref, row, start) * (1.0 / 9.0)
            tangent = box(three_ref, row, start) * (1.0 / 9.0)
            inverse = near(2, row, start) * far(2, row, start)
            scale = near(3, row, start) * far(3, row, start)
            cosine = sigma * inverse
            sine, inverse_sine, slope = arc(cosine)
            part = scale * sine * (1.0 / math.pi)
            values = part + slope * (sigma + tangent)
            turn = tangent * inverse_sine * (1.0 / math.pi)
            put(one_ref, row, start, slope)
            put(four_ref, row, start, slope + turn * inverse)
            q2_ref[0, row, start : start + CHUNK] = part - turn * cosine
            total = total + jnp.sum(values, axis=0)
        return total

    total = lax.fori_loop(0, SIDE, second_level, jnp.zeros((SUB, LANES), jnp.float32))
    kernel_ref[0] = total * (1.0 / pixels)

    def back(row, carry):
        for start in starts:
            inner = box(one_ref, row, start) * (1.0 / 9.0)
            energy = box(four_ref, row, start) * (1.0 / 9.0) + inner
            cosine = prod_ref[0, row, start : start + CHUNK]
            slope = q1_ref[0, row, start : start + CHUNK]
            scale = near(1, row, start) * far(1, row, start)
            square = (1.0 - cosine) * (1.0 + cosine)
            inverse_sine = lax.rsqrt(square)
            turn = inner * cosine * inverse_sine * (1.0 / math.pi)
            put(two_ref, row, start, (inner + energy) * slope + turn)
            q1_ref[0, row, start : start + CHUNK] = scale * (
                energy * (square * inverse_sine) * (1.0 / math.pi) - turn * cosine
            )
        return carry

    lax.fori_loop(0, SIDE, back, 0)

    def last(row, carry):
        for start in starts:
            prod_ref[0, row, start : start + CHUNK] = box(two_ref, row, start) * (
                1.0 / (9.0 * channels)
            )
        return carry

    lax.fori_loop(0, SIDE, last, 0)


def pair_maps(first, second):
    channels, groups = first.shape[:2]
    plane = pltpu.VMEM((SIDE + 2, SIDE + 2, SUB, LANES), jnp.float32)
    big = jax.ShapeDtypeStruct((groups, SIDE, SIDE, SUB, LANES), jnp.float32)
    big_spec = pl.BlockSpec((1, SIDE, SIDE, SUB, LANES), lambda g: (g, 0, 0, 0, 0))
    return pl.pallas_call(
        maps_kernel,
        grid=(groups,),
        out_shape=(jax.ShapeDtypeStruct((groups, SUB, LANES), jnp.float32), big, big, big),
        in_specs=[
            pl.BlockSpec((channels, 1, SIDE, SUB, LANES), lambda g: (0, g, 0, 0, 0)),
            pl.BlockSpec((channels, SIDE, SIDE, LANES), lambda g: (0, 0, 0, 0)),
        ],
        out_specs=(pl.BlockSpec((1, SUB, LANES), lambda g: (g, 0, 0)), big_spec, big_spec, big_spec),
        scratch_shapes=[
            pltpu.VMEM((4, SIDE, SUB, LANES), jnp.float32),
            pltpu.VMEM((4, SIDE, SIDE, LANES), jnp.float32),
            plane, plane, plane, plane,
        ],
        compiler_params=pltpu.CompilerParams(vmem_limit_bytes=58 * 1024 * 1024),
        name="pair_maps",
    )(first, second)


ROWS = 4


def contract_kernel(weight_ref, first_ref, second_ref, prod_ref, q1_ref, q2_ref, out_ref, d_ref, a_ref, b_ref):
    channels, groups = first_ref.shape[:2]
    step = pl.program_id(0)

    def body(index, carry):
        row = step * ROWS + index
        for start in range(0, SIDE, CHUNK):
            window = slice(start, start + CHUNK)
            totals = [None] * (channels + 2)

            def add(slot, value):
                totals[slot] = value if totals[slot] is None else totals[slot] + value

            for group in range(groups):
                weight = weight_ref[group][None]
                part = prod_ref[group, index, window] * weight
                for channel in range(channels):
                    block = first_ref[channel, group, row]
                    near = jnp.stack(
                        [
                            jnp.broadcast_to(block[:, x : x + 1], (SUB, LANES))
                            for x in range(start, start + CHUNK)
                        ]
                    )
                    add(channel, part * near)
                add(channels, q1_ref[group, index, window] * weight)
                add(channels + 1, q2_ref[group, index, window] * weight)
            for channel in range(channels):
                d_ref[channel, row, window, :] = jnp.sum(totals[channel], axis=1)
            a_ref[row, window, :] = jnp.sum(totals[channels], axis=1)
            b_ref[row, window, :] = jnp.sum(totals[channels + 1], axis=1)
        return carry

    lax.fori_loop(0, ROWS, body, 0)

    @pl.when(step == SIDE // ROWS - 1)
    def _():
        square = second_ref[0] * second_ref[0]
        for channel in range(1, channels):
            square = square + second_ref[channel] * second_ref[channel]
        first_diag = plane_window(square * (1.0 / channels))
        energy, rate = self_energy(first_diag)
        second_diag = plane_window(energy)
        grad_two = b_ref[...] * (0.5 / (second_diag + JITTER))
        grad_one = a_ref[...] * (0.5 / (first_diag + JITTER)) + plane_window(grad_two) * rate
        a_ref[...] = plane_window(grad_one) * (2.0 / channels)
        strips = SIDE * SIDE // LANES
        rows = SIDE // strips
        for channel in range(channels):
            for strip in range(strips):
                window = slice(strip * rows, (strip + 1) * rows)
                value = d_ref[channel, window] + a_ref[window] * second_ref[channel, window]
                out_ref[channel * strips + strip] = value.reshape(LANES, LANES).T


def contract(weight, first, second, prod, q1, q2):
    channels, groups = first.shape[:2]
    big_spec = pl.BlockSpec((groups, ROWS, SIDE, SUB, LANES), lambda s: (0, s, 0, 0, 0))
    strips = channels * SIDE * SIDE // LANES
    return pl.pallas_call(
        contract_kernel,
        grid=(SIDE // ROWS,),
        out_shape=jax.ShapeDtypeStruct((strips, LANES, LANES), jnp.float32),
        in_specs=[
            pl.BlockSpec(weight.shape, lambda s: (0, 0, 0)),
            pl.BlockSpec(first.shape, lambda s: (0, 0, 0, 0, 0)),
            pl.BlockSpec(second.shape, lambda s: (0, 0, 0, 0)),
            big_spec, big_spec, big_spec,
        ],
        out_specs=pl.BlockSpec((strips, LANES, LANES), lambda s: (0, 0, 0)),
        scratch_shapes=[
            pltpu.VMEM((channels, SIDE, SIDE, LANES), jnp.float32),
            pltpu.VMEM((SIDE, SIDE, LANES), jnp.float32),
            pltpu.VMEM((SIDE, SIDE, LANES), jnp.float32),
        ],
        compiler_params=pltpu.CompilerParams(vmem_limit_bytes=50 * 1024 * 1024),
        name="contract",
    )(weight, first, second, prod, q1, q2)


def bits_of(row_count, col_count):
    rows = row_count.bit_length() - 1
    cols = col_count.bit_length() - 1
    order = [("row", 0)] if rows else []
    return order + [("col", k) for k in range(cols)] + [("row", k) for k in range(1, rows)]


def flip(index, bit):
    size = 1 << bit
    mine = lax.rem(lax.div(index, jnp.int32(size)), jnp.int32(2))
    return mine, index + size - 2 * size * mine


def partner_of(axis, bit):
    row, col = lax.axis_index("row"), lax.axis_index("col")
    if axis == "row":
        mine, row = flip(row, bit)
    else:
        mine, col = flip(col, bit)
    return mine, (row, col)


def greet(partners):
    barrier = pltpu.get_barrier_semaphore()
    for unused, device in partners:
        pl.semaphore_signal(barrier, inc=1, device_id=device, device_id_type=MESH)
    pl.semaphore_wait(barrier, len(partners))


def sum_kernel(bits, value_ref, out_ref, send_ref, recv_ref, send_sem, recv_sem):
    partners = [partner_of(*item) for item in bits]
    greet(partners)
    total = value_ref[...]
    for step, (unused, device) in enumerate(partners):
        send_ref[step] = total
        copy = pltpu.make_async_remote_copy(
            src_ref=send_ref.at[step], dst_ref=recv_ref.at[step],
            send_sem=send_sem.at[step], recv_sem=recv_sem.at[step],
            device_id=device, device_id_type=MESH,
        )
        copy.start()
        copy.wait()
        total = total + recv_ref[step]
    out_ref[...] = total


def sum_all(value, bits, collective):
    steps = len(bits)
    return pl.pallas_call(
        functools.partial(sum_kernel, bits),
        out_shape=jax.ShapeDtypeStruct(value.shape, value.dtype),
        in_specs=[pl.BlockSpec(memory_space=pltpu.VMEM)],
        out_specs=pl.BlockSpec(memory_space=pltpu.VMEM),
        scratch_shapes=[
            pltpu.VMEM((steps,) + value.shape, value.dtype),
            pltpu.VMEM((steps,) + value.shape, value.dtype),
            pltpu.SemaphoreType.DMA((steps,)),
            pltpu.SemaphoreType.DMA((steps,)),
        ],
        compiler_params=pltpu.CompilerParams(collective_id=collective, has_side_effects=True),
        name="sum_all",
    )(value)


def gather_kernel(bits, value_ref, out_ref, hold_ref, send_sem, recv_sem):
    partners = [partner_of(*item) for item in bits]
    greet(partners)
    place = 0
    for step, (mine, unused) in enumerate(partners):
        place = place + (mine << step)
    hold_ref[place] = value_ref[...]
    for step, (unused, device) in enumerate(partners):
        size = 1 << step
        window = pl.ds(lax.div(place, jnp.int32(size)) * size, size)
        copy = pltpu.make_async_remote_copy(
            src_ref=hold_ref.at[window], dst_ref=hold_ref.at[window],
            send_sem=send_sem.at[step], recv_sem=recv_sem.at[step],
            device_id=device, device_id_type=MESH,
        )
        copy.start()
        copy.wait()
    out_ref[...] = hold_ref[...]


def gather_all(value, bits, collective):
    steps = len(bits)
    shape = (1 << steps,) + value.shape
    return pl.pallas_call(
        functools.partial(gather_kernel, bits),
        out_shape=jax.ShapeDtypeStruct(shape, value.dtype),
        in_specs=[pl.BlockSpec(memory_space=pltpu.VMEM)],
        out_specs=pl.BlockSpec(memory_space=pltpu.VMEM),
        scratch_shapes=[
            pltpu.VMEM(shape, value.dtype),
            pltpu.SemaphoreType.DMA((steps,)),
            pltpu.SemaphoreType.DMA((steps,)),
        ],
        compiler_params=pltpu.CompilerParams(collective_id=collective, has_side_effects=True),
        name="gather_all",
    )(value)


def aligned(start):
    return start if isinstance(start, int) else pl.multiple_of(start, SUB)


def reduce_kernel(bits, value_ref, out_ref, hold_ref, recv_ref, back_ref, send_sem, recv_sem, back_send, back_recv):
    strips, support = value_ref.shape[:2]
    partners = [partner_of(*item) for item in bits]
    greet(partners)
    hold_ref[...] = value_ref[...]
    lead, size = strips, support
    lead_at, size_at = 0, 0
    offset = 0
    undo = []
    cols = sum(axis == "col" for axis, unused in bits)
    for step, (axis, unused) in enumerate(bits):
        mine, device = partners[step]
        if axis == "col" or (size // 2) % SUB == 0:
            kind = 1
            half = size // 2
            keep_at, send_at = size_at + mine * half, size_at + (1 - mine) * half
            keep = (pl.ds(lead_at, lead), pl.ds(aligned(keep_at), half))
            send = (pl.ds(lead_at, lead), pl.ds(aligned(send_at), half))
        elif lead % 2 == 0:
            kind = 0
            half = lead // 2
            keep_at, send_at = lead_at + mine * half, lead_at + (1 - mine) * half
            keep = (pl.ds(keep_at, half), pl.ds(aligned(size_at), size))
            send = (pl.ds(send_at, half), pl.ds(aligned(size_at), size))
        else:
            kind = None
            keep = send = (pl.ds(lead_at, lead), pl.ds(aligned(size_at), size))
        if kind == 1:
            shape = (lead, half)
        elif kind == 0:
            shape = (half, size)
        else:
            shape = (lead, size)
        land = (pl.ds(offset, shape[0]), pl.ds(0, shape[1]))
        offset += shape[0]
        copy = pltpu.make_async_remote_copy(
            src_ref=hold_ref.at[send], dst_ref=recv_ref.at[land],
            send_sem=send_sem.at[step], recv_sem=recv_sem.at[step],
            device_id=device, device_id_type=MESH,
        )
        copy.start()
        copy.wait()
        hold_ref[keep] = hold_ref[keep] + recv_ref[land]
        if kind == 1:
            size, size_at = half, keep_at
        elif kind == 0:
            lead, lead_at = half, keep_at
        if axis == "row" and kind is not None:
            undo.append((device, keep))
    window = (pl.ds(lead_at, lead), pl.ds(aligned(size_at), size))
    back_ref[window] = hold_ref[window]
    for step, (device, keep) in enumerate(reversed(undo)):
        copy = pltpu.make_async_remote_copy(
            src_ref=back_ref.at[keep], dst_ref=back_ref.at[keep],
            send_sem=back_send.at[step], recv_sem=back_recv.at[step],
            device_id=device, device_id_type=MESH,
        )
        copy.start()
        copy.wait()
    panel = support >> cols
    start = lax.axis_index("col") * panel
    out_ref[...] = back_ref[:, pl.ds(pl.multiple_of(start, SUB), panel)]


def reduce_panels(value, row_count, col_count, collective):
    strips, support = value.shape[:2]
    rows, cols = row_count.bit_length() - 1, col_count.bit_length() - 1
    bits = [("col", k) for k in reversed(range(cols))] + [("row", k) for k in range(rows)]
    steps = len(bits)
    panel = support // col_count
    return pl.pallas_call(
        functools.partial(reduce_kernel, bits),
        out_shape=jax.ShapeDtypeStruct((strips, panel, LANES), value.dtype),
        in_specs=[pl.BlockSpec(memory_space=pltpu.VMEM)],
        out_specs=pl.BlockSpec(memory_space=pltpu.VMEM),
        scratch_shapes=[
            pltpu.VMEM(value.shape, value.dtype),
            pltpu.VMEM((strips * steps, max(support // 2, SUB), LANES), value.dtype),
            pltpu.VMEM(value.shape, value.dtype),
            pltpu.SemaphoreType.DMA((steps,)),
            pltpu.SemaphoreType.DMA((steps,)),
            pltpu.SemaphoreType.DMA((steps,)),
            pltpu.SemaphoreType.DMA((steps,)),
        ],
        compiler_params=pltpu.CompilerParams(
            collective_id=collective, has_side_effects=True, vmem_limit_bytes=40 * 1024 * 1024
        ),
        name="reduce_panels",
    )(value)


def order_matrix(panel_order, blocks):
    return (panel_order[:, None] == jnp.arange(blocks, dtype=jnp.int32)[None, :]).astype(
        jnp.float32
    )


def ridge_factor(kernel):
    number = kernel.shape[0]
    ridge_term = RIDGE * jnp.trace(kernel) / number
    return jnp.linalg.cholesky(kernel + ridge_term * jnp.eye(number, dtype=kernel.dtype))


def ridge_solve(factor, rhs):
    middle = lax.linalg.triangular_solve(factor, rhs, left_side=True, lower=True)
    return lax.linalg.triangular_solve(factor, middle, left_side=True, lower=True, transpose_a=True)


def local(target_images, target_labels, support_images, support_labels, panel_order):
    highest = lax.Precision.HIGHEST
    row_count = lax.axis_size("row")
    col_count = lax.axis_size("col")
    devices = row_count * col_count
    panel_size, channels, pixels = support_images.shape
    support = panel_size * col_count
    targets_dev = target_images.shape[0]
    bits = bits_of(row_count, col_count)
    place = 0
    for step, (axis, bit) in enumerate(bits):
        place = place + (((lax.axis_index(axis) >> bit) & 1) << step)

    gathered = lax.all_gather(support_images, "col", axis=0, tiled=True)
    own_rows = -(-support // devices)
    owners = support // own_rows
    own_start = lax.rem(place, owners) * own_rows
    own = lax.dynamic_slice_in_dim(gathered, own_start, own_rows, 0)
    count = targets_dev + own_rows
    groups = -(-count // SUB)
    first = jnp.concatenate([target_images, own], axis=0)
    first = jnp.pad(first, ((0, groups * SUB - count), (0, 0), (0, 0)))
    first = first.reshape(groups, SUB, channels, SIDE, SIDE).transpose(2, 0, 3, 1, 4)
    first = jnp.pad(first, ((0, 0),) * 4 + ((0, LANES - SIDE),))
    second = gathered.transpose(1, 2, 0).reshape(channels, SIDE, SIDE, support)

    values, prod, q1, q2 = pair_maps(first, second)
    values = values.reshape(groups * SUB, support)
    kernel_ts = values[:targets_dev]
    mine = values[targets_dev:count]
    block = jnp.pad(mine, ((0, -own_rows % SUB), (0, 0)))
    kernel_ss = gather_all(block, bits, 1)[:owners, :own_rows].reshape(support, support)

    wanted = (target_labels[:, None] == jnp.arange(CLASSES, dtype=jnp.int32)[None, :]).astype(
        jnp.float32
    ) - 0.1
    matrix = order_matrix(panel_order, support)
    stored_labels = jnp.dot(matrix, support_labels, precision=highest)
    factor = ridge_factor(kernel_ss)
    alphas = ridge_solve(factor, stored_labels)
    residual = jnp.dot(kernel_ts, alphas, precision=highest) - wanted
    partial = jnp.dot(residual.T, kernel_ts, precision=highest)
    squared = jnp.full((1, support), jnp.sum(residual * residual), jnp.float32)
    message = jnp.concatenate([partial, squared], axis=0)
    message = jnp.pad(message, ((0, -(CLASSES + 1) % SUB), (0, 0)))
    summed = sum_all(message, bits, 2)
    alpha_grad = summed[:CLASSES].T
    total_targets = targets_dev * devices
    loss_value = 0.5 * summed[CLASSES, 0] / total_targets
    adjoint = ridge_solve(factor, alpha_grad)
    own_alphas = lax.dynamic_slice_in_dim(alphas, own_start, own_rows, 0)
    own_adjoint = lax.dynamic_slice_in_dim(adjoint, own_start, own_rows, 0)
    ids = own_start + jnp.arange(own_rows, dtype=jnp.int32)
    diagonal = (ids[:, None] == jnp.arange(support, dtype=jnp.int32)[None, :]).astype(jnp.float32)
    kss_grad = (
        -jnp.dot(own_adjoint, alphas.T, precision=highest)
        - jnp.dot(own_alphas, adjoint.T, precision=highest)
        - 2.0 * RIDGE / support * jnp.sum(adjoint * alphas) * diagonal
    )
    kss_grad = jnp.where(place < owners, kss_grad, 0.0)
    kts_grad = jnp.dot(residual, alphas.T, precision=highest)
    weight = jnp.concatenate([kts_grad, kss_grad], axis=0) * (1.0 / pixels)
    weight = jnp.pad(weight, ((0, groups * SUB - count), (0, 0))).reshape(groups, SUB, support)

    gradient = contract(weight, first, second, prod, q1, q2)
    panel = reduce_panels(gradient, row_count, col_count, 3)
    grad_support = (
        panel.reshape(channels, pixels // LANES, panel_size, LANES)
        .transpose(2, 0, 1, 3)
        .reshape(panel_size, channels, pixels)
    )
    return (loss_value, grad_support, jnp.dot(matrix.T, adjoint, precision=highest))


def solution(mesh):
    placed = (P(("row", "col"), None, None), P(("row", "col")), P("col", None, None), P(), P())
    return jax.shard_map(
        local,
        mesh=mesh,
        in_specs=placed,
        out_specs=(P(), P("col", None, None), P()),
        check_vma=False,
    )
```

time: 1000 us -> 295 us (0.29)
  other arithmetic: 451 us -> 26.7 us
  local copies, waits for them, and re-layouts: 220 us -> 9.8 us
  Pallas kernels: 0 us -> 202 us
  waiting for transfers between devices: 222 us -> 31.3 us
  blocking collectives: 41.1 us -> 0 us
  matrix products: 35.4 us -> 7.09 us
    add x33 -> x1, other arithmetic: 216 us -> 0.01 us  [local(): ids = own_start + jnp.arange(own_rows, dtype=jnp.int32)]
    psum x2 -> x0, waiting for transfers between devices: 208 us -> none  [the longest x1 131 us: local(): summed = lax.psum(gradient, ('row', 'col'))]
    pallas_call x0 -> x5, Pallas kernels: none -> 202 us  [the longest x1 98.2 us: pair_maps(): pl.pallas_call(maps_kernel, grid=(groups,), out_shape=(jax.ShapeDtypeStru...]
    slice x48 -> x2, local copies, waits for them, and re-layouts: 155 us -> 1.98 us  [the longest x1 1.19 us: local(): loss_value = 0.5 * summed[CLASSES, 0] / total_targets]
    reduce_sum x13 -> x0, other arithmetic: 133 us -> none  [the longest x2 75.6 us: pair_pullback(): grad_q1 = jnp.sum(grad_scale1 * first_scales / (2.0 * first_far), axis=0)]
    div x28 -> x0, other arithmetic: 42.4 us -> none  [the longest x6 15 us: rectify(): scales * (jnp.sqrt(1.0 - cosine * cosine) + (math.pi - angles) * cosine)]
    psum x1 -> x0, blocking collectives: 41.1 us -> none  [local(): lax.psum((jnp.dot(kernel_ts.T, residual, precision=highest), jnp.sum(resi...]
    dot_general x6 -> x5, matrix products: 33.1 us -> 3.14 us  [the longest x1 0.89 us: local(): partial = jnp.dot(residual.T, kernel_ts, precision=highest)]
  transfers between devices with their start and end apart: 3 -> 1, of which waited for: 3 -> 1; matrix products, arithmetic and copies ran while one was open for 6% -> 0% of each run, Pallas kernels for 0% -> 0%
where the time goes in v1:
time: 295 us; the launch traced here: 294 us
  Pallas kernels  202 us (68%)
  waiting for transfers between devices  31.3 us (11%)
  other arithmetic  26.7 us (9%)
  between operations  17.3 us (6%)
  local copies, waits for them, and re-layouts  9.8 us (3%)
  matrix products  7.09 us (2%)
    pallas_call x1, Pallas kernels, pair_maps(): pl.pallas_call(maps_kernel, grid=(groups,), out_shape=(jax.ShapeDtypeStru...  98.2 us
    pallas_call x1, Pallas kernels, reduce_panels(): pl.pallas_call(functools.partial(reduce_kernel, bits), out_shape=jax.Shap...  48.2 us
    all_gather x1, waiting for transfers between devices, local(): gathered = lax.all_gather(support_images, 'col', axis=0, tiled=True)  30.6 us
    pallas_call x1, Pallas kernels, contract(): pl.pallas_call(contract_kernel, grid=(SIDE // ROWS,), out_shape=jax.Shape...  24.1 us
    pallas_call x1, Pallas kernels, gather_all(): pl.pallas_call(functools.partial(gather_kernel, bits), out_shape=jax.Shap...  17.8 us
    pallas_call x1, Pallas kernels, sum_all(): pl.pallas_call(functools.partial(sum_kernel, bits), out_shape=jax.ShapeDt...  13.6 us
    another operation x3, other arithmetic, ridge_factor(): jnp.linalg.cholesky(kernel + ridge_term * jnp.eye(number, dtype=kernel.dt...  12.4 us
    another operation x2, other arithmetic, ridge_solve(): lax.linalg.triangular_solve(factor, middle, left_side=True, lower=True, t...  10.5 us
  transfers between devices with their start and end apart: 1, of which 1 were waited for; matrix products, arithmetic and copies ran while one was open for 0% of the time, Pallas kernels for 0%

profile of v1, /device:TPU:0, one launch (start us, length us, event | category | flops | bytes accessed | tf_op | source)
XLA Modules:
  0.0 294.2 jit_solution(2486362628333366190)
XLA Ops:
  7.2 0.0 copy-start
  7.2 0.0 all-gather.2.cloned.1.call-start
  7.2 0.7 all-gather.2.cloned.1.call-update
  8.0 0.0 copy-done
  8.0 0.9 fusion.13
  8.9 30.6 %all-gather.2.cloned.1.call-done = f32[128,3,1024]{2,0,1:T(8,128)} async-done(((f32[64,3,1024]{2,0,1:T(8,128)}), f32[128,3,1024]{2,0,1:T(8,128)}) %all-gather.2.cloned.1.call-update) | async-done | bytes 1572880 | tf_op jit(solution)/shard_map/all_gather | solution.py:557
  39.5 0.9 constant_dynamic-slice_fusion
  40.4 1.0 select_maximum_fusion
  41.4 0.4 reshape.64
  41.8 0.7 copy.18
  42.5 3.0 %copy.12 = f32[3,1024,128]{2,1,0:T(8,128)} copy(f32[3,1024,128]{1,2,0:T(8,128)} %bitcast.67) | data formatting | bytes 3145728 | tf_op jit(solution)/shard_map/transpose | solution.py:568
  45.5 1.1 pad.22.first_ref
  46.6 0.0 copy-start.3
  46.6 0.0 copy-start.2
  46.6 98.2 %pair_maps.1 = (f32[3,8,128]{2,1,0:T(8,128)}, f32[3,32,32,8,128]{4,3,2,1,0:T(8,128)}, f32[3,32,32,8,128]{4,3,2,1,0:T(8,128)}, f32[3,32,32,8,128]{4,3,2,1,0:T(8,128)}) custom-call(f32[3,3,32,8,128]{4,3,2,1,0:T(8,128)} %pad.22.first_ref, f32[3,32,32,128]{3,2,1,0:T(8,128)} %bitcast.64), custom_call_target="tpu_custom_call" | custom-call | tf_op jit(solution)/shard_map/pair_maps/pallas_call | solution.py:228
  144.8 0.0 copy-start.1
  144.8 0.8 slice.34
  145.6 0.6 pad.23.value_ref
  146.2 17.8 %gather_all.1 = f32[32,8,128]{2,1,0:T(8,128)} custom-call(f32[8,128]{1,0:T(8,128)} %pad.23.value_ref), custom_call_target="tpu_custom_call" | custom-call | tf_op jit(solution)/shard_map/gather_all/pallas_call | solution.py:417
  164.0 1.6 select_reduce_fusion.1
  166.3 0.1 copy.13
  166.4 11.7 %cholesky.19 = f32[128,128]{1,0:T(8,128)S(1)} custom-call(f32[128,128]{1,0:T(8,128)S(1)} %fusion.11), custom_call_target="Cholesky" | custom-call | tf_op jit(solution)/shard_map/jit(cholesky)/cholesky | solution.py:536
  178.1 0.6 compare_reduce_fusion
  178.8 0.7 fusion.2
  179.4 9.8 %custom-call.12 = f32[1,128,128]{1,2,0:T(8,128)S(1)} custom-call(f32[1,128,128]{2,1,0:T(8,128)S(1)} %fusion.2), custom_call_target="InvertDiagBlocksLowerTriangular" | custom-call | tf_op jit(solution)/shard_map/triangular_solve/custom-call.2 | solution.py:541
  189.3 0.3 fusion.7
  189.6 0.2 fusion.9
  189.8 0.0 copy-done.3
  189.8 1.5 multiply_reduce_fusion.1
  191.3 0.9 fusion.17
  192.1 0.1 fusion.27
  192.3 1.3 pad_select_fusion.value_ref
  193.5 13.6 %sum_all.1 = f32[16,128]{1,0:T(8,128)} custom-call(f32[16,128]{1,0:T(8,128)} %pad_select_fusion.value_ref), custom_call_target="tpu_custom_call" | custom-call | tf_op jit(solution)/shard_map/sum_all/pallas_call | solution.py:378
  207.1 1.2 slice.32
  208.3 1.0 fusion.3
  209.3 0.9 multiply_reduce_fusion
  210.2 0.3 convolution_negate_fusion
  210.4 0.0 copy-done.2
  210.4 0.8 fusion.12
  211.9 0.3 fusion.1
  212.2 0.0 copy-done.1
  212.2 24.1 %contract.1.value_ref = f32[24,128,128]{2,1,0:T(8,128)S(1)} custom-call(f32[3,8,128]{2,1,0:T(8,128)S(1)} %pad_bitcast_fusion.weight_ref, f32[3,3,32,8,128]{4,3,2,1,0:T(8,128)S(1)} %copy-done.1, f32[3,32,32,128]{3,2,1,0:T(8,128)} %bitcast.65, f32[3,32,32,8,128]{4,3,2,1,0:T(8,128)} %get-tuple-element.10.prod_ref, ...), custom_call_target="tpu_custom_call" | custom-call | tf_op jit(solution)/shard_map/contract/pallas_call | solution.py:309
  236.4 48.2 %reduce_panels.1 = f32[24,64,128]{2,1,0:T(8,128)S(1)} custom-call(f32[24,128,128]{2,1,0:T(8,128)S(1)} %contract.1.value_ref), custom_call_target="tpu_custom_call" | custom-call | tf_op jit(solution)/shard_map/reduce_panels/pallas_call | solution.py:506
  284.6 1.0 copy.19
  (7 shorter events, 0.1 us)
Async XLA Ops:
  7.2 0.8 copy-start
  7.2 32.3 %all-gather.2.cloned.1.call-start = ((), (), s32[]{:S(2)}) async-start(), calls=%async_computation | async-start | bytes 2359296 | tf_op jit(solution)/shard_map/all_gather | solution.py:557
  46.6 143.2 %copy-start.3 = (s32[16]{0:T(128)S(1)}, s32[16]{0:T(128)}, u32[]{:S(2)}) copy-start(s32[16]{0:T(128)} %param.10) | copy-start | bytes 196
  46.6 163.8 %copy-start.2 = (s32[128]{0:T(128)S(1)}, s32[128]{0:T(128)}, u32[]{:S(2)}) copy-start(s32[128]{0:T(128)} %param.13) | copy-start | bytes 1540
  144.8 67.5 %copy-start.1 = (f32[3,3,32,8,128]{4,3,2,1,0:T(8,128)S(1)}, f32[3,3,32,8,128]{4,3,2,1,0:T(8,128)}, u32[]{:S(2)}) copy-start(f32[3,3,32,8,128]{4,3,2,1,0:T(8,128)} %pad.22.first_ref) | copy-start | bytes 3538948
Sparse Core Ops, SparseCore 0:
  9.6 29.8 all-gather.1

commit v2 on v1

--- a/solution.py
+++ b/solution.py
@@ -433,74 +433,108 @@
     return start if isinstance(start, int) else pl.multiple_of(start, SUB)
 
 
+CHUNKS = 2
+
+
 def reduce_kernel(bits, value_ref, out_ref, hold_ref, recv_ref, back_ref, send_sem, recv_sem, back_send, back_recv):
     strips, support = value_ref.shape[:2]
+    panel = back_ref.shape[1]
+    steps = len(bits)
     partners = [partner_of(*item) for item in bits]
     greet(partners)
-    hold_ref[...] = value_ref[...]
-    lead, size = strips, support
-    lead_at, size_at = 0, 0
-    offset = 0
-    undo = []
-    cols = sum(axis == "col" for axis, unused in bits)
-    for step, (axis, unused) in enumerate(bits):
+    chunks = [
+        {"lead": strips // CHUNKS, "lead_at": k * (strips // CHUNKS), "size": support, "size_at": 0, "rel": 0, "undo": []}
+        for k in range(CHUNKS)
+    ]
+    offset = [0]
+
+    def begin(number, step):
+        chunk = chunks[number]
+        lead, size = chunk["lead"], chunk["size"]
+        lead_at, size_at, rel = chunk["lead_at"], chunk["size_at"], chunk["rel"]
+        axis = bits[step][0]
         mine, device = partners[step]
-        if axis == "col" or (size // 2) % SUB == 0:
-            kind = 1
+        wide = size > panel
+        if axis == "col" or (not wide and (size // 2) % SUB == 0):
             half = size // 2
             keep_at, send_at = size_at + mine * half, size_at + (1 - mine) * half
             keep = (pl.ds(lead_at, lead), pl.ds(aligned(keep_at), half))
             send = (pl.ds(lead_at, lead), pl.ds(aligned(send_at), half))
+            shape = (lead, half)
+            chunk["size"], chunk["size_at"] = half, keep_at
+            chunk["rel"] = rel + mine * half if axis == "row" else 0
         elif lead % 2 == 0:
-            kind = 0
             half = lead // 2
             keep_at, send_at = lead_at + mine * half, lead_at + (1 - mine) * half
             keep = (pl.ds(keep_at, half), pl.ds(aligned(size_at), size))
             send = (pl.ds(send_at, half), pl.ds(aligned(size_at), size))
+            shape = (half, size)
+            chunk["lead"], chunk["lead_at"] = half, keep_at
         else:
-            kind = None
             keep = send = (pl.ds(lead_at, lead), pl.ds(aligned(size_at), size))
-        if kind == 1:
-            shape = (lead, half)
-        elif kind == 0:
-            shape = (half, size)
-        else:
             shape = (lead, size)
-        land = (pl.ds(offset, shape[0]), pl.ds(0, shape[1]))
-        offset += shape[0]
+        if axis == "row" and shape != (lead, size):
+            extent = min(chunk["size"], panel)
+            chunk["undo"].append(
+                (device, (pl.ds(chunk["lead_at"], chunk["lead"]), pl.ds(aligned(chunk["rel"]), extent)))
+            )
+        land = (pl.ds(offset[0], shape[0]), pl.ds(0, shape[1]))
+        offset[0] += shape[0]
+        source = value_ref if step == 0 else hold_ref
+        slot = number * steps + step
         copy = pltpu.make_async_remote_copy(
-            src_ref=hold_ref.at[send], dst_ref=recv_ref.at[land],
-            send_sem=send_sem.at[step], recv_sem=recv_sem.at[step],
+            src_ref=source.at[send], dst_ref=recv_ref.at[land],
+            send_sem=send_sem.at[slot], recv_sem=recv_sem.at[slot],
             device_id=device, device_id_type=MESH,
         )
         copy.start()
+        chunk["open"] = (copy, source, keep, land)
+
+    def end(number):
+        copy, source, keep, land = chunks[number]["open"]
         copy.wait()
-        hold_ref[keep] = hold_ref[keep] + recv_ref[land]
-        if kind == 1:
-            size, size_at = half, keep_at
-        elif kind == 0:
-            lead, lead_at = half, keep_at
-        if axis == "row" and kind is not None:
-            undo.append((device, keep))
-    window = (pl.ds(lead_at, lead), pl.ds(aligned(size_at), size))
-    back_ref[window] = hold_ref[window]
-    for step, (device, keep) in enumerate(reversed(undo)):
-        copy = pltpu.make_async_remote_copy(
-            src_ref=back_ref.at[keep], dst_ref=back_ref.at[keep],
-            send_sem=back_send.at[step], recv_sem=back_recv.at[step],
-            device_id=device, device_id_type=MESH,
-        )
-        copy.start()
-        copy.wait()
-    panel = support >> cols
-    start = lax.axis_index("col") * panel
-    out_ref[...] = back_ref[:, pl.ds(pl.multiple_of(start, SUB), panel)]
+        hold_ref[keep] = source[keep] + recv_ref[land]
+
+    for step in range(steps):
+        for number in range(CHUNKS):
+            if step:
+                end(number)
+            begin(number, step)
+    for number in range(CHUNKS):
+        end(number)
+        chunk = chunks[number]
+        inner = (pl.ds(chunk["lead_at"], chunk["lead"]), pl.ds(aligned(chunk["rel"]), chunk["size"]))
+        outer = (pl.ds(chunk["lead_at"], chunk["lead"]), pl.ds(aligned(chunk["size_at"]), chunk["size"]))
+        back_ref[inner] = hold_ref[outer]
+        chunk["copy"] = None
+        chunk["undo"].reverse()
+        undo(chunk, number * steps, 0, back_ref, back_send, back_recv)
+    for step in range(1, len(chunks[0]["undo"])):
+        for number in range(CHUNKS):
+            chunks[number]["copy"].wait()
+            undo(chunks[number], number * steps, step, back_ref, back_send, back_recv)
+    for number in range(CHUNKS):
+        if chunks[number]["copy"] is not None:
+            chunks[number]["copy"].wait()
+    out_ref[...] = back_ref[...]
+
+
+def undo(chunk, base, step, back_ref, back_send, back_recv):
+    if step >= len(chunk["undo"]):
+        return
+    device, window = chunk["undo"][step]
+    chunk["copy"] = pltpu.make_async_remote_copy(
+        src_ref=back_ref.at[window], dst_ref=back_ref.at[window],
+        send_sem=back_send.at[base + step], recv_sem=back_recv.at[base + step],
+        device_id=device, device_id_type=MESH,
+    )
+    chunk["copy"].start()
 
 
 def reduce_panels(value, row_count, col_count, collective):
     strips, support = value.shape[:2]
     rows, cols = row_count.bit_length() - 1, col_count.bit_length() - 1
-    bits = [("col", k) for k in reversed(range(cols))] + [("row", k) for k in range(rows)]
+    bits = [("row", 0)] + [("col", k) for k in reversed(range(cols))] + [("row", k) for k in range(1, rows)]
     steps = len(bits)
     panel = support // col_count
     return pl.pallas_call(
@@ -510,12 +544,12 @@
         out_specs=pl.BlockSpec(memory_space=pltpu.VMEM),
         scratch_shapes=[
             pltpu.VMEM(value.shape, value.dtype),
-            pltpu.VMEM((strips * steps, max(support // 2, SUB), LANES), value.dtype),
-            pltpu.VMEM(value.shape, value.dtype),
-            pltpu.SemaphoreType.DMA((steps,)),
-            pltpu.SemaphoreType.DMA((steps,)),
-            pltpu.SemaphoreType.DMA((steps,)),
-            pltpu.SemaphoreType.DMA((steps,)),
+            pltpu.VMEM((strips * steps // 2, support, LANES), value.dtype),
+            pltpu.VMEM((strips, panel, LANES), value.dtype),
+            pltpu.SemaphoreType.DMA((CHUNKS * steps,)),
+            pltpu.SemaphoreType.DMA((CHUNKS * steps,)),
+            pltpu.SemaphoreType.DMA((CHUNKS * steps,)),
+            pltpu.SemaphoreType.DMA((CHUNKS * steps,)),
         ],
         compiler_params=pltpu.CompilerParams(
             collective_id=collective, has_side_effects=True, vmem_limit_bytes=40 * 1024 * 1024
@@ -524,21 +558,118 @@
     )(value)
 
 
+def panels_kernel(cols, panel_ref, all_ref, second_ref, hold_ref, send_sem, recv_sem):
+    strips, panel = panel_ref.shape[:2]
+    half = strips // 2
+    partners = [partner_of("col", k) for k in range(cols)] + [partner_of("row", 0)]
+    greet(partners)
+    col = lax.axis_index("col")
+    mine = pl.ds(partners[-1][0] * half, half)
+    hold_ref[mine, pl.ds(aligned(col * panel), panel)] = panel_ref[mine]
+    for step, (unused, device) in enumerate(partners):
+        window = (mine,)
+        if step < cols:
+            size = 1 << step
+            start = lax.div(col, jnp.int32(size)) * (size * panel)
+            window = (mine, pl.ds(aligned(start), size * panel))
+        copy = pltpu.make_async_remote_copy(
+            src_ref=hold_ref.at[window], dst_ref=hold_ref.at[window],
+            send_sem=send_sem.at[step], recv_sem=recv_sem.at[step],
+            device_id=device, device_id_type=MESH,
+        )
+        copy.start()
+        copy.wait()
+
+    def turn(strip, carry):
+        block = hold_ref[strip]
+        all_ref[strip] = block
+        second_ref[strip] = block.T
+        return carry
+
+    lax.fori_loop(0, strips, turn, 0)
+
+
+def gather_panels(panels, col_count, collective):
+    strips, panel = panels.shape[:2]
+    support = panel * col_count
+    cols = col_count.bit_length() - 1
+    return pl.pallas_call(
+        functools.partial(panels_kernel, cols),
+        out_shape=(
+            jax.ShapeDtypeStruct((strips, support, LANES), panels.dtype),
+            jax.ShapeDtypeStruct((strips, LANES, support), panels.dtype),
+        ),
+        in_specs=[pl.BlockSpec(memory_space=pltpu.VMEM)],
+        out_specs=(pl.BlockSpec(memory_space=pltpu.VMEM), pl.BlockSpec(memory_space=pltpu.VMEM)),
+        scratch_shapes=[
+            pltpu.VMEM((strips, support, LANES), panels.dtype),
+            pltpu.SemaphoreType.DMA((cols + 1,)),
+            pltpu.SemaphoreType.DMA((cols + 1,)),
+        ],
+        compiler_params=pltpu.CompilerParams(
+            collective_id=collective, has_side_effects=True, vmem_limit_bytes=24 * 1024 * 1024
+        ),
+        name="gather_panels",
+    )(panels)
+
+
+def exact_dot(left, right):
+    return jnp.dot(left, right, precision=lax.Precision.HIGHEST, preferred_element_type=jnp.float32)
+
+
+def solve_kernel(ss_ref, ts_ref, wanted_ref, labels_ref, inverse_ref, ridged_ref, alphas_ref, residual_ref, message_ref):
+    number = ss_ref.shape[0]
+    rows = lax.broadcasted_iota(jnp.int32, (number, number), 0)
+    lanes = lax.broadcasted_iota(jnp.int32, (number, number), 1)
+    kernel = ss_ref[...]
+    trace = jnp.sum(jnp.where(rows == lanes, kernel, 0.0))
+    ridged = kernel + jnp.where(rows == lanes, RIDGE * trace / number, 0.0)
+    ridged_ref[...] = ridged
+    lane = lax.broadcasted_iota(jnp.int32, (SUB, number), 1)
+    sublane = lax.broadcasted_iota(jnp.int32, (SUB, number), 0)
+    blocks = [ridged[k : k + SUB] for k in range(0, number, SUB)]
+    for k in range(number):
+        home, inner = divmod(k, SUB)
+        row = blocks[home][inner : inner + 1]
+        line = jnp.where(lane[:1] == k, 1.0, row) * (1.0 / row[:, k : k + 1])
+        here = lane == k
+        blocks = [jnp.where(here, 0.0, block) - block[:, k : k + 1] * line for block in blocks]
+        blocks[home] = jnp.where(sublane == inner, line, blocks[home])
+    inverse = jnp.concatenate(blocks, axis=0)
+    inverse_ref[...] = inverse
+    labels = labels_ref[...]
+    alphas = exact_dot(inverse, labels)
+    alphas = alphas + exact_dot(inverse, labels - exact_dot(ridged, alphas))
+    alphas_ref[...] = alphas
+    residual = exact_dot(ts_ref[...], alphas) - wanted_ref[...]
+    residual_ref[...] = residual
+    partial = lax.dot_general(
+        residual, ts_ref[...], (((0,), (0,)), ((), ())),
+        precision=lax.Precision.HIGHEST, preferred_element_type=jnp.float32,
+    )
+    classes = residual.shape[1]
+    spare = message_ref.shape[0] - classes
+    squared = jnp.sum(residual * residual)
+    message_ref[...] = jnp.concatenate([partial, jnp.broadcast_to(squared, (spare, number))], axis=0)
+
+
+def solve(kernel_ss, kernel_ts, wanted, labels):
+    number, classes = labels.shape
+    targets = kernel_ts.shape[0]
+    tall = -(-(classes + 1) // SUB) * SUB
+    shapes = [(number, number), (number, number), (number, classes), (targets, classes), (tall, number)]
+    return pl.pallas_call(
+        solve_kernel,
+        out_shape=tuple(jax.ShapeDtypeStruct(shape, jnp.float32) for shape in shapes),
+        compiler_params=pltpu.CompilerParams(vmem_limit_bytes=16 * 1024 * 1024),
+        name="solve",
+    )(kernel_ss, kernel_ts, wanted, labels)
+
+
 def order_matrix(panel_order, blocks):
     return (panel_order[:, None] == jnp.arange(blocks, dtype=jnp.int32)[None, :]).astype(
         jnp.float32
     )
-
-
-def ridge_factor(kernel):
-    number = kernel.shape[0]
-    ridge_term = RIDGE * jnp.trace(kernel) / number
-    return jnp.linalg.cholesky(kernel + ridge_term * jnp.eye(number, dtype=kernel.dtype))
-
-
-def ridge_solve(factor, rhs):
-    middle = lax.linalg.triangular_solve(factor, rhs, left_side=True, lower=True)
-    return lax.linalg.triangular_solve(factor, middle, left_side=True, lower=True, transpose_a=True)
 
 
 def local(target_images, target_labels, support_images, support_labels, panel_order):
@@ -554,18 +685,21 @@
     for step, (axis, bit) in enumerate(bits):
         place = place + (((lax.axis_index(axis) >> bit) & 1) << step)
 
-    gathered = lax.all_gather(support_images, "col", axis=0, tiled=True)
+    strips = channels * pixels // LANES
+    panels = support_images.reshape(panel_size, strips, LANES).transpose(1, 0, 2)
+    gathered, second = gather_panels(panels, col_count, 0)
+    second = second.reshape(channels, SIDE, SIDE, support)
     own_rows = -(-support // devices)
     owners = support // own_rows
     own_start = lax.rem(place, owners) * own_rows
-    own = lax.dynamic_slice_in_dim(gathered, own_start, own_rows, 0)
+    own = lax.dynamic_slice_in_dim(gathered, own_start, own_rows, 1)
+    own = own.transpose(1, 0, 2).reshape(own_rows, channels, pixels)
     count = targets_dev + own_rows
     groups = -(-count // SUB)
     first = jnp.concatenate([target_images, own], axis=0)
     first = jnp.pad(first, ((0, groups * SUB - count), (0, 0), (0, 0)))
     first = first.reshape(groups, SUB, channels, SIDE, SIDE).transpose(2, 0, 3, 1, 4)
     first = jnp.pad(first, ((0, 0),) * 4 + ((0, LANES - SIDE),))
-    second = gathered.transpose(1, 2, 0).reshape(channels, SIDE, SIDE, support)
 
     values, prod, q1, q2 = pair_maps(first, second)
     values = values.reshape(groups * SUB, support)
@@ -579,18 +713,14 @@
     ) - 0.1
     matrix = order_matrix(panel_order, support)
     stored_labels = jnp.dot(matrix, support_labels, precision=highest)
-    factor = ridge_factor(kernel_ss)
-    alphas = ridge_solve(factor, stored_labels)
-    residual = jnp.dot(kernel_ts, alphas, precision=highest) - wanted
-    partial = jnp.dot(residual.T, kernel_ts, precision=highest)
-    squared = jnp.full((1, support), jnp.sum(residual * residual), jnp.float32)
-    message = jnp.concatenate([partial, squared], axis=0)
-    message = jnp.pad(message, ((0, -(CLASSES + 1) % SUB), (0, 0)))
+    inverse, ridged, alphas, residual, message = solve(kernel_ss, kernel_ts, wanted, stored_labels)
     summed = sum_all(message, bits, 2)
     alpha_grad = summed[:CLASSES].T
     total_targets = targets_dev * devices
     loss_value = 0.5 * summed[CLASSES, 0] / total_targets
-    adjoint = ridge_solve(factor, alpha_grad)
+    adjoint = jnp.dot(inverse, alpha_grad, precision=highest)
+    missing = alpha_grad - jnp.dot(ridged, adjoint, precision=highest)
+    adjoint = adjoint + jnp.dot(inverse, missing, precision=highest)
     own_alphas = lax.dynamic_slice_in_dim(alphas, own_start, own_rows, 0)
     own_adjoint = lax.dynamic_slice_in_dim(adjoint, own_start, own_rows, 0)
     ids = own_start + jnp.arange(own_rows, dtype=jnp.int32)

time: 295 us -> 241 us (0.82)
  waiting for transfers between devices: 31.3 us -> 0 us
  other arithmetic: 26.7 us -> 0.77 us
  Pallas kernels: 202 us -> 219 us
  between operations: 17.3 us -> 3.25 us
    all_gather x1 -> x0, waiting for transfers between devices: 30.6 us -> none  [local(): gathered = lax.all_gather(support_images, 'col', axis=0, tiled=True)]
    pallas_call x0 -> x2, Pallas kernels: none -> 29.3 us  [the longest x1 17.2 us: gather_panels(): pl.pallas_call(functools.partial(panels_kernel, cols), out_shape=(jax.Sha...]
    another operation x5 -> x0, other arithmetic: 22.9 us -> none  [the longest x3 12.4 us: ridge_factor(): jnp.linalg.cholesky(kernel + ridge_term * jnp.eye(number, dtype=kernel.dt...]
    pallas_call x1, Pallas kernels: 48.2 us -> 36.1 us  [reduce_panels(): pl.pallas_call(functools.partial(reduce_kernel, bits), out_shape=jax.Shap...]
    unnamed x8 -> x13, local copies, waits for them, and re-layouts: 0.02 us -> 3.43 us
    transpose x1 -> x0, local copies, waits for them, and re-layouts: 3.02 us -> none  [local(): second = gathered.transpose(1, 2, 0).reshape(channels, SIDE, SIDE, support)]
  transfers between devices with their start and end apart: 1 -> 0, of which waited for: 1 -> 0; matrix products, arithmetic and copies ran while one was open for 0% -> 0% of each run, Pallas kernels for 0% -> 0%
where the time goes in v2:
time: 241 us; the launch traced here: 240 us
  Pallas kernels  219 us (91%)
  local copies, waits for them, and re-layouts  11.5 us (5%)
  matrix products  4.99 us (2%)
  between operations  3.25 us (1%)
    pallas_call x1, Pallas kernels, pair_maps(): pl.pallas_call(maps_kernel, grid=(groups,), out_shape=(jax.ShapeDtypeStru...  98.2 us
    pallas_call x1, Pallas kernels, reduce_panels(): pl.pallas_call(functools.partial(reduce_kernel, bits), out_shape=jax.Shap...  36.1 us
    pallas_call x1, Pallas kernels, contract(): pl.pallas_call(contract_kernel, grid=(SIDE // ROWS,), out_shape=jax.Shape...  24.1 us
    pallas_call x1, Pallas kernels, gather_all(): pl.pallas_call(functools.partial(gather_kernel, bits), out_shape=jax.Shap...  18.5 us
    pallas_call x1, Pallas kernels, gather_panels(): pl.pallas_call(functools.partial(panels_kernel, cols), out_shape=(jax.Sha...  17.2 us
    pallas_call x1, Pallas kernels, sum_all(): pl.pallas_call(functools.partial(sum_kernel, bits), out_shape=jax.ShapeDt...  13.2 us
    pallas_call x1, Pallas kernels, solve(): pl.pallas_call(solve_kernel, out_shape=tuple((jax.ShapeDtypeStruct(shape,...  12.1 us

profile of v2, /device:TPU:0, one launch (start us, length us, event | category | flops | bytes accessed | tf_op | source)
XLA Modules:
  0.0 239.9 jit_solution(1352707579732634967)
XLA Ops:
  0.6 0.0 copy-start
  0.7 0.7 convert_add_fusion.wanted_ref
  1.4 0.0 copy-done
  1.4 0.9 fusion.3.labels_ref
  2.3 1.7 copy.12
  4.0 0.4 reshape.42
  4.4 0.0 copy-start.4
  4.4 0.2 copy.27
  4.6 17.2 %gather_panels.1 = (f32[24,128,128]{2,1,0:T(8,128)S(1)}, f32[24,128,128]{2,1,0:T(8,128)S(1)}) custom-call(f32[24,64,128]{2,1,0:T(8,128)S(1)} %bitcast.41), custom_call_target="tpu_custom_call" | custom-call | tf_op jit(solution)/shard_map/gather_panels/pallas_call | solution.py:596
  21.8 0.0 copy-start.2
  21.8 1.1 copy-done.2
  22.9 0.0 copy-done.4
  23.0 0.4 reshape.44
  23.4 0.7 copy.25
  24.1 1.1 pad.17.first_ref
  25.2 0.0 copy-start.5
  25.2 0.0 copy-start.1
  25.2 98.2 %pair_maps.1 = (f32[3,8,128]{2,1,0:T(8,128)}, f32[3,32,32,8,128]{4,3,2,1,0:T(8,128)}, f32[3,32,32,8,128]{4,3,2,1,0:T(8,128)}, f32[3,32,32,8,128]{4,3,2,1,0:T(8,128)}) custom-call(f32[3,3,32,8,128]{4,3,2,1,0:T(8,128)} %pad.17.first_ref, f32[3,32,32,128]{3,2,1,0:T(8,128)} %bitcast.39), custom_call_target="tpu_custom_call" | custom-call | tf_op jit(solution)/shard_map/pair_maps/pallas_call | solution.py:228
  123.5 0.7 slice.24
  124.1 0.6 pad.18.value_ref
  124.7 0.7 slice_bitcast_fusion.ts_ref
  125.4 18.5 %gather_all.1 = f32[32,8,128]{2,1,0:T(8,128)} custom-call(f32[8,128]{1,0:T(8,128)} %pad.18.value_ref), custom_call_target="tpu_custom_call" | custom-call | tf_op jit(solution)/shard_map/gather_all/pallas_call | solution.py:417
  143.9 0.9 slice.19
  144.8 12.1 %solve.1 = (f32[128,128]{1,0:T(8,128)S(1)}, f32[128,128]{1,0:T(8,128)S(1)}, f32[128,10]{1,0:T(8,128)S(1)}, f32[16,10]{1,0:T(8,128)S(1)}, f32[16,128]{1,0:T(8,128)S(1)}) custom-call(f32[128,128]{1,0:T(8,128)S(1)} %bitcast.43, f32[16,128]{1,0:T(8,128)S(1)} %slice_bitcast_fusion.ts_ref, f32[16,10]{1,0:T(8,128)S(1)} %convert_add_fusion.wanted_ref, ...), custom_call_target="tpu_custom_call" | custom-call | tf_op jit(solution)/shard_map/solve/pallas_call | solution.py:661
  157.0 0.0 copy-start.3
  157.0 0.6 copy-done.3
  157.6 13.2 %sum_all.1 = f32[16,128]{1,0:T(8,128)} custom-call(f32[16,128]{1,0:T(8,128)} %copy-done.3), custom_call_target="tpu_custom_call" | custom-call | tf_op jit(solution)/shard_map/sum_all/pallas_call | solution.py:378
  170.8 1.2 slice.22
  172.6 0.9 fusion.6
  173.5 0.9 convolution_subtract_fusion
  174.4 0.2 fusion.12
  174.6 0.1 copy.16
  174.8 0.8 multiply_reduce_fusion
  176.2 0.2 convolution_negate_fusion
  176.4 0.2 fusion.1
  176.7 0.0 copy-done.5
  176.7 0.9 fusion.2
  177.6 0.0 copy-done.1
  177.6 24.1 %contract.1.value_ref = f32[24,128,128]{2,1,0:T(8,128)S(1)} custom-call(f32[3,8,128]{2,1,0:T(8,128)S(1)} %pad_bitcast_fusion.weight_ref, f32[3,3,32,8,128]{4,3,2,1,0:T(8,128)S(1)} %copy-done.1, f32[3,32,32,128]{3,2,1,0:T(8,128)} %bitcast.40, f32[3,32,32,8,128]{4,3,2,1,0:T(8,128)} %get-tuple-element.22.prod_ref, ...), custom_call_target="tpu_custom_call" | custom-call | tf_op jit(solution)/shard_map/contract/pallas_call | solution.py:309
  201.7 36.1 %reduce_panels.1 = f32[24,64,128]{2,1,0:T(8,128)S(1)} custom-call(f32[24,128,128]{2,1,0:T(8,128)S(1)} %contract.1.value_ref), custom_call_target="tpu_custom_call" | custom-call | tf_op jit(solution)/shard_map/reduce_panels/pallas_call | solution.py:540
  237.8 1.0 copy.26
  (5 shorter events, 0.1 us)
Async XLA Ops:
  0.6 0.8 copy-start
  4.4 18.5 %copy-start.4 = (f32[16,3,1024]{2,0,1:T(8,128)S(1)}, f32[16,3,1024]{2,0,1:T(8,128)}, u32[]{:S(2)}) copy-start(f32[16,3,1024]{2,0,1:T(8,128)} %param.5) | copy-start | bytes 589828
  21.8 1.1 copy-start.2
  25.2 151.5 %copy-start.5 = (s32[128]{0:T(128)S(1)}, s32[128]{0:T(128)}, u32[]{:S(2)}) copy-start(s32[128]{0:T(128)} %param.9) | copy-start | bytes 1540
  25.2 152.4 %copy-start.1 = (f32[3,3,32,8,128]{4,3,2,1,0:T(8,128)S(1)}, f32[3,3,32,8,128]{4,3,2,1,0:T(8,128)}, u32[]{:S(2)}) copy-start(f32[3,3,32,8,128]{4,3,2,1,0:T(8,128)} %pad.17.first_ref) | copy-start | bytes 3538948
  157.0 0.6 copy-start.3
